TPU v7x, 32 devices: a whole 2x2x4 slice. The times are simulated.
32 devices in a mesh: wide: 8 (over z, x), narrow: 4 (over y, core).
Axes of the slice: x: 2, y: 2, z: 4, core: 2. Of those that a mesh axis runs over, the one named last changes fastest.
Arguments:
- params: float32 [3129344], P(('wide', 'narrow')), may hold values from -2 to 2
- first_moment: float32 [3129344], P(('wide', 'narrow')), may hold values from -0.00390625 to 0.00390625
- second_moment: float32 [3129344], P(('wide', 'narrow')), may hold values from 2.746582e-09 to 4.3945313e-08
- ct_image: bfloat16 [16, 32, 32], P('wide', 'narrow'), may hold values from -10 to 10
- labels: int32 [16, 32, 32], P('wide', 'narrow'), may hold values from 0 to 2
- valid_mask: int32 [16, 32, 32], P('wide', 'narrow'), may hold values from 0 to 1
Outputs:
- new_params: float32 [3129344], P(('wide', 'narrow'))
- new_first: float32 [3129344], P(('wide', 'narrow'))
- new_second: float32 [3129344], P(('wide', 'narrow'))
- loss_sum: float32 [], replicated
- valid_count: float32 [], replicated
All inputs are finite; a program needn't handle non-finite values.
Results may differ from a plain program's by a relative error of at most 0.0077.
Values may be sent and summed in bfloat16 or wider, within the bound.
A program may use at most 128 MiB of HBM per device.

v0:
```python
import jax
import jax.numpy as jnp
from jax import lax
from jax.sharding import PartitionSpec as P

C1 = 128
C2 = 256
GATE = 64
CLASSES = 3
STEP = 10


EPS_NORM = 1e-05
BETA_ONE = 0.9
BETA_TWO = 0.999
EPS_ADAM = 1e-06
DECAY_RATE = 0.01
LEARN_RATE = 0.3


def extended(cells, sides, width):
    for axis, dim in sides:
        count = lax.axis_size(axis)
        ends = count - 1
        head = lax.slice_in_dim(cells, 0, width, axis=dim)
        tail = lax.slice_in_dim(cells, cells.shape[dim] - width, cells.shape[dim], axis=dim)
        cells = jnp.concatenate(
            [
                lax.ppermute(tail, axis, [(i, (i + 1) % count) for i in range(ends)]),
                cells,
                lax.ppermute(head, axis, [((i + 1) % count, i) for i in range(ends)]),
            ],
            axis=dim,
        )
    return cells


def layout_table():
    return [
        (27, 1, C1),
        (27, C1, C1),
        (27, C1, C2),
        (C1, GATE),
        (C2, GATE),
        (GATE,),
        (27, C1 + C2, C1),
        (27, C1, C1),
        (C1 + 1, CLASSES),
        (4 * C1 + C2,),
        (4 * C1 + C2,),
    ]


def table_lengths():
    lengths = []
    for tensor_shape in layout_table():
        length = 1
        for extent in tensor_shape:
            length = length * extent
        lengths.append(length)
    return lengths


def unpack_weights(flat_weights):
    pieces = []
    offset = 0
    for tensor_shape, length in zip(layout_table(), table_lengths()):
        pieces.append(flat_weights[offset : offset + length].reshape(tensor_shape))
        offset = offset + length
    return pieces


def fine_pad(volume):
    framed = extended(volume, (("wide", 0), ("narrow", 1)), 1)
    return jnp.pad(framed, ((0, 0), (0, 0), (1, 1), (0, 0)))


def coarse_pad(volume):
    framed = extended(volume, (("wide", 0),), 1)
    return jnp.pad(framed, ((0, 0), (1, 1), (1, 1), (0, 0)))


def tap_window(padded, tap_id, extent):
    along_x, along_y, along_z = (tap_id // 9, tap_id // 3 % 3, tap_id % 3)
    window = padded[
        along_x : along_x + extent[0], along_y : along_y + extent[1], along_z : along_z + extent[2]
    ]
    return window.reshape(-1, padded.shape[3])


def apply_taps(padded, kernel, extent):
    result = jnp.zeros((extent[0] * extent[1] * extent[2], kernel.shape[2]), jnp.float32)
    for tap_id in range(27):
        result = result + jnp.dot(
            tap_window(padded, tap_id, extent), kernel[tap_id], preferred_element_type=jnp.float32
        )
    return result.reshape(extent[0], extent[1], extent[2], kernel.shape[2])


def kernel_grad(padded, grad_low, extent):
    flat_grad = grad_low.reshape(-1, grad_low.shape[3])
    blocks = []
    for tap_id in range(27):
        blocks.append(
            lax.dot_general(
                tap_window(padded, tap_id, extent),
                flat_grad,
                (((0,), (0,)), ((), ())),
                preferred_element_type=jnp.float32,
            )
        )
    return jnp.stack(blocks)


def flip_kernel(kernel):
    return jnp.swapaxes(kernel[::-1], 1, 2)


def pool_sum(volume):
    sx, sy, sz, width_c = volume.shape
    return jnp.sum(volume.reshape(sx // 2, 2, sy // 2, 2, sz // 2, 2, width_c), axis=(1, 3, 5))


def upsample(volume):
    return jnp.repeat(jnp.repeat(jnp.repeat(volume, 2, 0), 2, 1), 2, 2)


def silu_grad(pre_act):
    squashed = jax.nn.sigmoid(pre_act)
    return squashed * (1.0 + pre_act * (1.0 - squashed))


def fine_sums(parts):
    return lax.psum(parts, ("wide", "narrow"))


def coarse_sums(parts):
    return lax.psum(parts, "wide")


def norm_forward(raw, gain_v, bias_v, voxels, summer, extras):
    row_view = raw.reshape(-1, raw.shape[3])
    summed = summer((jnp.sum(row_view, 0), jnp.sum(row_view * row_view, 0)) + extras)
    mean_v = summed[0] / voxels
    spread = summed[1] / voxels - mean_v * mean_v
    inverse = lax.rsqrt(spread + EPS_NORM)
    normed = (raw - mean_v) * inverse
    return (normed, inverse, normed * gain_v + bias_v, summed[2:])


def norm_backward(grad_out, normed, inverse, gain_v, voxels, summer, extras):
    grad_rows = grad_out.reshape(-1, grad_out.shape[3])
    normed_rows = normed.reshape(-1, normed.shape[3])
    local_shift = jnp.sum(grad_rows, 0)
    local_gain = jnp.sum(grad_rows * normed_rows, 0)
    summed = summer((local_shift, local_gain) + extras)
    grad_raw = inverse * gain_v * (grad_out - summed[0] / voxels - normed * (summed[1] / voxels))
    return (grad_raw, local_shift, local_gain, summed[2:])


def on_device(params, first_moment, second_moment, ct_image, labels, valid_mask):
    shard_len = params.shape[0]
    n_wide = lax.axis_size("wide")
    n_narrow = lax.axis_size("narrow")
    place = lax.axis_index(("wide", "narrow"))
    gathered = lax.all_gather(params.astype(jnp.bfloat16), ("wide", "narrow"), axis=0, tiled=True)
    w_in, w_enc, w_mid, w_x, w_g, w_psi, w_dec1, w_dec2, w_head, gains, shifts = unpack_weights(
        gathered
    )
    gain_all = gains.astype(jnp.float32)
    shift_all = shifts.astype(jnp.float32)
    bounds = [0, C1, 2 * C1, 2 * C1 + C2, 3 * C1 + C2, 4 * C1 + C2]

    def gain_at(layer_id):
        return gain_all[bounds[layer_id] : bounds[layer_id + 1]]

    def shift_at(layer_id):
        return shift_all[bounds[layer_id] : bounds[layer_id + 1]]

    depth, height, length = ct_image.shape
    fine_ext = (depth, height, length)
    coarse_ext = (depth // 2, height * n_narrow // 2, length // 2)
    own_ext = (depth // 2, height // 2, length // 2)
    voxels = float(depth * height * length * n_wide * n_narrow)
    coarse_voxels = voxels / 8.0
    valid_float = valid_mask.astype(jnp.float32)
    hot_labels = (labels[..., None] == jnp.arange(CLASSES, dtype=jnp.int32)).astype(jnp.float32)
    pad_entry = fine_pad(ct_image[..., None])
    raw_entry = apply_taps(pad_entry, w_in, fine_ext)
    hat_entry, inv_entry, pre_entry, counted = norm_forward(
        raw_entry, gain_at(0), shift_at(0), voxels, fine_sums, (jnp.sum(valid_float),)
    )
    valid_count = counted[0]
    act_entry = jax.nn.silu(pre_entry).astype(jnp.bfloat16)
    pad_encode = fine_pad(act_entry)
    raw_encode = apply_taps(pad_encode, w_enc, fine_ext)
    hat_encode, inv_encode, pre_encode, unused = norm_forward(
        raw_encode, gain_at(1), shift_at(1), voxels, fine_sums, ()
    )
    skip_out = jax.nn.silu(pre_encode)
    pooled = (pool_sum(skip_out) / 8.0).astype(jnp.bfloat16)
    pooled_all = lax.all_gather(pooled, "narrow", axis=1, tiled=True)
    pad_middle = coarse_pad(pooled_all)
    raw_middle = apply_taps(pad_middle, w_mid, coarse_ext)
    hat_middle, inv_middle, pre_middle, unused = norm_forward(
        raw_middle, gain_at(2), shift_at(2), coarse_voxels, coarse_sums, ()
    )
    row_start = lax.axis_index("narrow") * (height // 2)
    coarse_own = jax.nn.silu(
        lax.dynamic_slice_in_dim(pre_middle, row_start, height // 2, 1)
    ).astype(jnp.bfloat16)
    skip_low = skip_out.astype(jnp.bfloat16)
    gate_fine = jnp.einsum("xyzc,cd->xyzd", skip_low, w_x, preferred_element_type=jnp.float32)
    gate_coarse = jnp.einsum("xyzc,cd->xyzd", coarse_own, w_g, preferred_element_type=jnp.float32)
    mixed_in = gate_fine + upsample(gate_coarse)
    mixed = jax.nn.silu(mixed_in)
    psi_float = w_psi.astype(jnp.float32)
    attention = jax.nn.sigmoid(jnp.dot(mixed, psi_float, precision=lax.Precision.HIGHEST))
    gated = (skip_out * attention[..., None]).astype(jnp.bfloat16)
    joined = jnp.concatenate([gated, upsample(coarse_own)], -1)
    pad_decode = fine_pad(joined)
    raw_decode = apply_taps(pad_decode, w_dec1, fine_ext)
    hat_decode, inv_decode, pre_decode, unused = norm_forward(
        raw_decode, gain_at(3), shift_at(3), voxels, fine_sums, ()
    )
    act_decode = jax.nn.silu(pre_decode).astype(jnp.bfloat16)
    pad_final = fine_pad(act_decode)
    raw_final = apply_taps(pad_final, w_dec2, fine_ext)
    hat_final, inv_final, pre_final, unused = norm_forward(
        raw_final, gain_at(4), shift_at(4), voxels, fine_sums, ()
    )
    act_final = jax.nn.silu(pre_final).astype(jnp.bfloat16)
    logits = jnp.einsum(
        "xyzc,cd->xyzd", act_final, w_head[:C1], preferred_element_type=jnp.float32
    ) + w_head[C1].astype(jnp.float32)
    top_value = jnp.max(logits, -1, keepdims=True)
    log_total = top_value[..., 0] + jnp.log(jnp.sum(jnp.exp(logits - top_value), -1))
    picked = jnp.sum(logits * hot_labels, -1)
    loss_local = jnp.sum(valid_float * (log_total - picked))
    probs = jnp.exp(logits - log_total[..., None])
    grad_logits = (valid_float[..., None] * (probs - hot_labels) / valid_count).astype(jnp.bfloat16)
    head_grad = jnp.concatenate(
        [
            jnp.einsum("xyzc,xyzd->cd", act_final, grad_logits, preferred_element_type=jnp.float32),
            jnp.sum(grad_logits.astype(jnp.float32), (0, 1, 2))[None],
        ],
        0,
    )
    (head_grad,) = (head_grad,)
    grad_act = jnp.einsum(
        "xyzd,cd->xyzc", grad_logits, w_head[:C1], preferred_element_type=jnp.float32
    )
    grad_raw, shift_final, gain_final, lossy = norm_backward(
        grad_act * silu_grad(pre_final),
        hat_final,
        inv_final,
        gain_at(4),
        voxels,
        fine_sums,
        (loss_local,),
    )
    loss_sum = lossy[0]
    low_raw = grad_raw.astype(jnp.bfloat16)
    (dec2_grad,) = (kernel_grad(pad_final, low_raw, fine_ext),)
    grad_act = apply_taps(fine_pad(low_raw), flip_kernel(w_dec2), fine_ext)
    grad_raw, shift_decode, gain_decode, unused = norm_backward(
        grad_act * silu_grad(pre_decode), hat_decode, inv_decode, gain_at(3), voxels, fine_sums, ()
    )
    low_raw = grad_raw.astype(jnp.bfloat16)
    (dec1_grad,) = (kernel_grad(pad_decode, low_raw, fine_ext),)
    grad_joined = apply_taps(fine_pad(low_raw), flip_kernel(w_dec1), fine_ext)
    grad_gated = grad_joined[..., :C1]
    grad_coarse = pool_sum(grad_joined[..., C1:])
    grad_skip = grad_gated * attention[..., None]
    grad_attention = jnp.sum(grad_gated * skip_out, -1)
    grad_logit_att = grad_attention * attention * (1.0 - attention)
    psi_grad = jnp.einsum("xyzc,xyz->c", mixed, grad_logit_att, precision=lax.Precision.HIGHEST)
    grad_mixed = grad_logit_att[..., None] * psi_float * silu_grad(mixed_in)
    low_fine = grad_mixed.astype(jnp.bfloat16)
    low_gate_coarse = pool_sum(grad_mixed).astype(jnp.bfloat16)
    x_grad = jnp.einsum("xyzc,xyzd->cd", skip_low, low_fine, preferred_element_type=jnp.float32)
    grad_skip = grad_skip + jnp.einsum(
        "xyzd,cd->xyzc", low_fine, w_x, preferred_element_type=jnp.float32
    )
    g_grad = jnp.einsum(
        "xyzc,xyzd->cd", coarse_own, low_gate_coarse, preferred_element_type=jnp.float32
    )
    grad_coarse = grad_coarse + jnp.einsum(
        "xyzd,cd->xyzc", low_gate_coarse, w_g, preferred_element_type=jnp.float32
    )
    x_grad, g_grad, psi_grad = (x_grad, g_grad, psi_grad)
    coarse_all = lax.all_gather(
        grad_coarse.astype(jnp.bfloat16), "narrow", axis=1, tiled=True
    ).astype(jnp.float32)
    grad_pre_mid = coarse_all * silu_grad(pre_middle)
    grad_raw_mid, unused_shift, unused_gain, unused = norm_backward(
        grad_pre_mid, hat_middle, inv_middle, gain_at(2), coarse_voxels, coarse_sums, ()
    )
    grad_pre_own = lax.dynamic_slice_in_dim(grad_pre_mid, row_start, height // 2, 1)
    hat_own = lax.dynamic_slice_in_dim(hat_middle, row_start, height // 2, 1)
    shift_middle = jnp.sum(grad_pre_own, (0, 1, 2))
    gain_middle = jnp.sum(grad_pre_own * hat_own, (0, 1, 2))
    low_mid = grad_raw_mid.astype(jnp.bfloat16)
    own_low = lax.dynamic_slice_in_dim(low_mid, row_start, height // 2, 1)
    pad_own = lax.dynamic_slice_in_dim(pad_middle, row_start, height // 2 + 2, 1)
    (mid_grad,) = (kernel_grad(pad_own, own_low, own_ext),)
    grad_back = lax.dynamic_slice_in_dim(coarse_pad(low_mid), row_start, height // 2 + 2, 1)
    grad_pooled = apply_taps(grad_back, flip_kernel(w_mid), own_ext)
    grad_skip = grad_skip + upsample(grad_pooled) / 8.0
    grad_raw, shift_encode, gain_encode, unused = norm_backward(
        grad_skip * silu_grad(pre_encode), hat_encode, inv_encode, gain_at(1), voxels, fine_sums, ()
    )
    low_raw = grad_raw.astype(jnp.bfloat16)
    (enc_grad,) = (kernel_grad(pad_encode, low_raw, fine_ext),)
    grad_act = apply_taps(fine_pad(low_raw), flip_kernel(w_enc), fine_ext)
    grad_raw, shift_entry, gain_entry, unused = norm_backward(
        grad_act * silu_grad(pre_entry), hat_entry, inv_entry, gain_at(0), voxels, fine_sums, ()
    )
    in_grad = kernel_grad(pad_entry, grad_raw.astype(jnp.bfloat16), fine_ext)
    gain_grads = jnp.concatenate([gain_entry, gain_encode, gain_middle, gain_decode, gain_final])
    shift_grads = jnp.concatenate(
        [shift_entry, shift_encode, shift_middle, shift_decode, shift_final]
    )
    in_grad, gain_grads, shift_grads = (in_grad, gain_grads, shift_grads)
    devices = n_wide * n_narrow
    raw_len = sum(table_lengths())
    ordered = [
        in_grad,
        enc_grad,
        mid_grad,
        x_grad,
        g_grad,
        psi_grad,
        dec1_grad,
        dec2_grad,
        head_grad,
        gain_grads,
        shift_grads,
    ]
    flat_grad = jnp.concatenate(
        [member.reshape(-1) for member in ordered]
        + [jnp.zeros((shard_len * devices - raw_len,), jnp.float32)]
    )
    gradient = lax.psum_scatter(flat_grad, ("wide", "narrow"), scatter_dimension=0, tiled=True)
    new_first = BETA_ONE * first_moment + (1.0 - BETA_ONE) * gradient
    new_second = BETA_TWO * second_moment + (1.0 - BETA_TWO) * gradient * gradient
    update = (
        new_first
        / (1.0 - BETA_ONE**STEP)
        / (jnp.sqrt(new_second / (1.0 - BETA_TWO**STEP)) + EPS_ADAM)
        + DECAY_RATE * params
    )
    starts = [0]
    for length_v in table_lengths():
        starts.append(starts[-1] + length_v)
    seg_lower = jnp.array(starts, jnp.int32)
    seg_upper = jnp.array(starts[1:] + [shard_len * devices], jnp.int32)
    position = place * shard_len + lax.iota(jnp.int32, shard_len)
    member_map = (
        (position[:, None] >= seg_lower[None]) & (position[:, None] < seg_upper[None])
    ).astype(jnp.float32)
    weight_sq = jnp.dot(params * params, member_map, precision=lax.Precision.HIGHEST)
    update_sq = jnp.dot(update * update, member_map, precision=lax.Precision.HIGHEST)
    weight_sq, update_sq = lax.psum((weight_sq, update_sq), ("wide", "narrow"))
    trust_ratio = jnp.sqrt(weight_sq) / jnp.sqrt(update_sq)
    new_params = (
        params
        - LEARN_RATE * jnp.dot(member_map, trust_ratio, precision=lax.Precision.HIGHEST) * update
    )
    return (new_params, new_first, new_second, loss_sum, valid_count)


def solution(mesh):
    in_specs = (
        P(("wide", "narrow")),
        P(("wide", "narrow")),
        P(("wide", "narrow")),
        P("wide", "narrow", None),
        P("wide", "narrow", None),
        P("wide", "narrow", None),
    )
    out_specs = (P(("wide", "narrow")), P(("wide", "narrow")), P(("wide", "narrow")), P(), P())
    return jax.shard_map(
        on_device, mesh=mesh, in_specs=in_specs, out_specs=out_specs, check_vma=False
    )
```

profile of v0, /device:TPU:0, one launch (start us, length us, event | category | flops | bytes accessed | tf_op | source)
XLA Modules:
  0.0 1440.3 jit_solution(9235467086159178304)
XLA Ops:
  11.2 5.5 collective-permute-start
  48.1 61.7 %all-gather.5.cloned.1.call-done = bf16[32,1,97792]{2,1,0:T(2,128)(2,1)} async-done(((bf16[1,1,97792]{2,1,0:T(2,128)(2,1)}), bf16[32,1,97792]{2,1,0:T(2,128)(2,1)}) %all-gather.5.cloned.1.call-update) | async-done | bytes 6258704 | tf_op jit(solution)/shard_map/all_gather | solution.py:166
  109.8 120.6 %reduce.10 = bf16[32,97792]{1,0:T(8,128)(2,1)} reduce(bf16[32,1,97792]{2,1,0:T(2,128)(2,1)} %all-gather.5.cloned.1.call-done, bf16[]{:T(256)} %constant.123), dimensions={1}, to_apply=%all-gather.2.reduce_sub_computation | reduce | bytes 12517378 | tf_op jit(solution)/shard_map/all_gather | solution.py:166
  230.4 12.0 reshape.2548
  260.0 38.6 %all-reduce.18 = (f32[128]{0:T(128)S(1)}, f32[128]{0:T(128)S(1)}) all-reduce(f32[128]{0:T(128)S(1)} %get-tuple-element.20, f32[128]{0:T(128)S(1)} %get-tuple-element.19), channel_id=1, replica_groups=mesh['wide'=8,'narrow'=4] {'wide','narrow'}, use_global_device_ids=true, to_apply=%region_2.3 | all-reduce | flops 256 | bytes 2048 | tf_op jit(solution)/shard_map/psum | solution.py:134
  300.7 4.8 collective-permute-start.4
  343.2 43.3 %all-reduce.17 = (f32[128]{0:T(128)S(1)}, f32[128]{0:T(128)S(1)}) all-reduce(f32[128]{0:T(128)S(1)} %get-tuple-element.18, f32[128]{0:T(128)S(1)} %get-tuple-element.17), channel_id=1, replica_groups=mesh['wide'=8,'narrow'=4] {'wide','narrow'}, use_global_device_ids=true, to_apply=%region_6.7 | all-reduce | flops 256 | bytes 2048 | tf_op jit(solution)/shard_map/psum | solution.py:134
  386.7 5.6 all-gather
  423.1 20.4 %all-reduce.20 = (f32[256]{0:T(256)S(1)}, f32[256]{0:T(256)S(1)}) all-reduce(f32[256]{0:T(256)S(1)} %get-tuple-element.16, f32[256]{0:T(256)S(1)} %get-tuple-element.15), channel_id=1, replica_groups=mesh['wide'=8,'narrow'=4] {'wide'}, use_global_device_ids=true, to_apply=%region_13.14 | all-reduce | flops 512 | bytes 4096 | tf_op jit(solution)/shard_map/psum | solution.py:138
  494.1 42.7 %all-reduce.16 = (f32[128]{0:T(128)S(1)}, f32[128]{0:T(128)S(1)}) all-reduce(f32[128]{0:T(128)S(1)} %get-tuple-element.14, f32[128]{0:T(128)S(1)} %get-tuple-element.13), channel_id=1, replica_groups=mesh['wide'=8,'narrow'=4] {'wide','narrow'}, use_global_device_ids=true, to_apply=%region_15.16 | all-reduce | flops 256 | bytes 2048 | tf_op jit(solution)/shard_map/psum | solution.py:134
  538.6 4.8 collective-permute-start.14
  581.4 42.5 %all-reduce.15 = (f32[128]{0:T(128)S(1)}, f32[128]{0:T(128)S(1)}) all-reduce(f32[128]{0:T(128)S(1)} %get-tuple-element.12, f32[128]{0:T(128)S(1)} %get-tuple-element.11), channel_id=1, replica_groups=mesh['wide'=8,'narrow'=4] {'wide','narrow'}, use_global_device_ids=true, to_apply=%region_19.20 | all-reduce | flops 256 | bytes 2048 | tf_op jit(solution)/shard_map/psum | solution.py:134
  630.2 40.3 %psum.179 = f32[]{:T(128)} all-reduce(f32[]{:T(128)} %get-tuple-element.24), channel_id=1, replica_groups=mesh['wide'=8,'narrow'=4] {'wide','narrow'}, use_global_device_ids=true, to_apply=%region_25.26 | all-reduce | flops 1 | bytes 8 | tf_op jit(solution)/shard_map/psum | solution.py:134
  675.7 40.2 %all-reduce.14 = (f32[128]{0:T(128)S(1)}, f32[128]{0:T(128)S(1)}) all-reduce(f32[128]{0:T(128)S(1)} %fusion.261, f32[128]{0:T(128)S(1)} %get-tuple-element.422), channel_id=1, replica_groups=mesh['wide'=8,'narrow'=4] {'wide','narrow'}, use_global_device_ids=true, to_apply=%region_29.30 | all-reduce | flops 256 | bytes 2048 | tf_op jit(solution)/shard_map/psum | solution.py:134
  721.1 5.4 collective-permute-start.18
  752.4 41.8 %all-reduce.13 = (f32[128]{0:T(128)S(1)}, f32[128]{0:T(128)S(1)}) all-reduce(f32[128]{0:T(128)S(1)} %get-tuple-element.10, f32[128]{0:T(128)S(1)} %get-tuple-element.9), channel_id=1, replica_groups=mesh['wide'=8,'narrow'=4] {'wide','narrow'}, use_global_device_ids=true, to_apply=%region_33.34 | all-reduce | flops 256 | bytes 2048 | tf_op jit(solution)/shard_map/psum | solution.py:134
  797.0 4.9 collective-permute-start.22
  829.3 6.7 all-gather.1
  836.2 18.7 %all-reduce.19 = (f32[256]{0:T(256)S(1)}, f32[256]{0:T(256)S(1)}) all-reduce(f32[256]{0:T(256)S(1)} %fusion.260, f32[256]{0:T(256)S(1)} %get-tuple-element.55), channel_id=1, replica_groups=mesh['wide'=8,'narrow'=4] {'wide'}, use_global_device_ids=true, to_apply=%region_42.43 | all-reduce | flops 512 | bytes 4096 | tf_op jit(solution)/shard_map/psum | solution.py:138
  886.2 40.0 %all-reduce.12 = (f32[128]{0:T(128)S(1)}, f32[128]{0:T(128)S(1)}) all-reduce(f32[128]{0:T(128)S(1)} %fusion.259, f32[128]{0:T(128)S(1)} %get-tuple-element.425), channel_id=1, replica_groups=mesh['wide'=8,'narrow'=4] {'wide','narrow'}, use_global_device_ids=true, to_apply=%region_46.47 | all-reduce | flops 256 | bytes 2048 | tf_op jit(solution)/shard_map/psum | solution.py:134
  951.4 43.7 %all-reduce.11 = (f32[128]{0:T(128)}, f32[128]{0:T(128)}) all-reduce(f32[128]{0:T(128)} %get-tuple-element.8, f32[128]{0:T(128)} %get-tuple-element.7), channel_id=1, replica_groups=mesh['wide'=8,'narrow'=4] {'wide','narrow'}, use_global_device_ids=true, to_apply=%region_50.51 | all-reduce | flops 256 | bytes 2048 | tf_op jit(solution)/shard_map/psum | solution.py:134
  1031.7 115.9 %concatenate.222 = f32[3129344]{0:T(1024)} concatenate(f32[3456]{0:T(1024)S(1)} %bitcast.2830, f32[442368]{0:T(1024)} %bitcast.2603, f32[884736]{0:T(1024)S(1)} %bitcast.2579, f32[8192]{0:T(1024)} %reshape.2538, f32[16384]{0:T(1024)} %reshape.2539, f32[64]{0:T(128)} %convolution_bitcast_fusion.138, f32[1327104]{0:T(1024)} %bitcast.2589, f32[442368]{0:T(1024)} %bitcast.2602, ...), dimensions={0} | concatenate | bytes 25034752 | tf_op jit(solution)/shard_map/concatenate | solution.py:340
  1147.7 229.3 %all-reduce.23.cloned.1.call-done = f32[3129344]{0:T(1024)} async-done(((f32[3129344]{0:T(1024)}), f32[3129344]{0:T(1024)}) %all-reduce.23.cloned.1.call-update) | async-done | bytes 12517392
  1387.6 40.3 %all-reduce.10 = (f32[12]{0:T(128)S(1)}, f32[12]{0:T(128)S(1)}, f32[]{:T(128)}) all-reduce(f32[12]{0:T(128)S(1)} %fusion.187, f32[12]{0:T(128)S(1)} %fusion.186, f32[]{:T(128)} %get-tuple-element.23), channel_id=1, replica_groups=mesh['wide'=8,'narrow'=4] {'wide','narrow'}, use_global_device_ids=true, to_apply=%region_55.56 | all-reduce | flops 25 | bytes 200 | tf_op jit(solution)/shard_map/psum | solution.py:364
  (990 shorter events, 390.9 us)
Async XLA Ops:
  7.2 102.6 %all-gather.5.cloned.1.call-start = ((), (), s32[]{:S(2)}) async-start(), calls=%async_computation | async-start | bytes 12908544 | tf_op jit(solution)/shard_map/all_gather | solution.py:166
  9.2 1367.8 %all-reduce.23.cloned.1.call-start = ((), (), s32[]{:S(2)}) async-start(), calls=%async_computation.1 | async-start | bytes 25034752
  10.0 9.9 collective-permute-start.1
  11.2 8.6 collective-permute-start
  20.7 5.0 collective-permute-start.3
  299.4 11.8 collective-permute-start.5
  300.7 10.5 collective-permute-start.4
  392.3 23.8 %collective-permute-start.9 = (bf16[1,16,16,128]{3,2,1,0:T(8,128)(2,1)S(1)}, bf16[1,16,16,128]{3,2,1,0:T(8,128)(2,1)S(1)}, u32[]{:S(2)}, u32[]{:S(2)}) collective-permute-start(bf16[1,16,16,128]{3,2,1,0:T(8,128)(2,1)S(1)} %bitcast.2630), channel_id=1, source_target_pairs={{4,0},{8,4},{12,8},{16,12},{20,16},{24,20},{28,24},{5,1},{9,5},{13... | collective-permute-start | bytes 196616 | tf_op jit(solution)/shard_map/ppermute | solution.py:31
  393.6 22.5 %collective-permute-start.8 = (bf16[1,16,16,128]{3,2,1,0:T(8,128)(2,1)S(1)}, bf16[1,16,16,128]{3,2,1,0:T(8,128)(2,1)S(1)}, u32[]{:S(2)}, u32[]{:S(2)}) collective-permute-start(bf16[1,16,16,128]{3,2,1,0:T(8,128)(2,1)S(1)} %bitcast.2631), channel_id=1, source_target_pairs={{0,4},{4,8},{8,12},{12,16},{16,20},{20,24},{24,28},{1,5},{5,9},{9,... | collective-permute-start | bytes 196616 | tf_op jit(solution)/shard_map/ppermute | solution.py:29
  448.0 7.6 collective-permute-start.11
  449.3 7.7 collective-permute-start.10
  457.0 5.2 collective-permute-start.12
  537.4 9.9 collective-permute-start.15
  538.6 8.6 collective-permute-start.14
  719.8 17.5 %collective-permute-start.19 = (bf16[1,8,32,128]{3,2,1,0:T(8,128)(2,1)}, bf16[1,8,32,128]{3,2,1,0:T(8,128)(2,1)}, u32[]{:S(2)}, u32[]{:S(2)}) collective-permute-start(bf16[1,8,32,128]{3,2,1,0:T(8,128)(2,1)} %get-tuple-element.355), channel_id=1, source_target_pairs={{4,0},{8,4},{12,8},{16,12},{20,16},{24,20},{28,24},{5,1},{9,5},{13... | collective-permute-start | bytes 196616 | tf_op jit(solution)/shard_map/ppermute | solution.py:31
  721.1 16.2 %collective-permute-start.18 = (bf16[1,8,32,128]{3,2,1,0:T(8,128)(2,1)}, bf16[1,8,32,128]{3,2,1,0:T(8,128)(2,1)}, u32[]{:S(2)}, u32[]{:S(2)}) collective-permute-start(bf16[1,8,32,128]{3,2,1,0:T(8,128)(2,1)} %get-tuple-element.354), channel_id=1, source_target_pairs={{0,4},{4,8},{8,12},{12,16},{16,20},{20,24},{24,28},{1,5},{5,9},{9,... | collective-permute-start | bytes 196616 | tf_op jit(solution)/shard_map/ppermute | solution.py:29
  738.0 5.5 collective-permute-start.21
  795.7 15.6 %collective-permute-start.23 = (bf16[1,8,32,128]{3,2,1,0:T(8,128)(2,1)S(1)}, bf16[1,8,32,128]{3,2,1,0:T(8,128)(2,1)S(1)}, u32[]{:S(2)}, u32[]{:S(2)}) collective-permute-start(bf16[1,8,32,128]{3,2,1,0:T(8,128)(2,1)S(1)} %get-tuple-element.351), channel_id=1, source_target_pairs={{4,0},{8,4},{12,8},{16,12},{20,16},{24,20},{28,24},{5,1},{9,5},{13... | collective-permute-start | bytes 196616 | tf_op jit(solution)/shard_map/ppermute | solution.py:31
  797.0 14.3 collective-permute-start.22
  811.3 4.8 collective-permute-start.25
  855.0 17.5 %collective-permute-start.26 = (bf16[1,16,16,256]{3,2,1,0:T(8,128)(2,1)S(1)}, bf16[1,16,16,256]{3,2,1,0:T(8,128)(2,1)S(1)}, u32[]{:S(2)}, u32[]{:S(2)}) collective-permute-start(bf16[1,16,16,256]{3,2,1,0:T(8,128)(2,1)S(1)} %multiply_convert_fusion.3), channel_id=1, source_target_pairs={{0,4},{4,8},{8,12},{12,16},{16,20},{20,24},{24,28},{1,5},{5,9},{9,... | collective-permute-start | bytes 393224 | tf_op jit(solution)/shard_map/ppermute | solution.py:29
  857.4 15.2 %collective-permute-start.27 = (bf16[1,16,16,256]{3,2,1,0:T(8,128)(2,1)S(1)}, bf16[1,16,16,256]{3,2,1,0:T(8,128)(2,1)S(1)}, u32[]{:S(2)}, u32[]{:S(2)}) collective-permute-start(bf16[1,16,16,256]{3,2,1,0:T(8,128)(2,1)S(1)} %multiply_convert_fusion.3), channel_id=1, source_target_pairs={{4,0},{8,4},{12,8},{16,12},{20,16},{24,20},{28,24},{5,1},{9,5},{13... | collective-permute-start | bytes 393224 | tf_op jit(solution)/shard_map/ppermute | solution.py:31
  926.5 12.3 collective-permute-start.29
  927.8 11.0 collective-permute-start.28
  (159 other events, 4945.9 us)
Sparse Core Ops, SparseCore 0:
  11.4 98.3 all-gather.4
  1147.8 229.1 all-reduce.22
where the time goes:
time: 1460 us; the launch traced here: 1440 us
  blocking collectives  465 us (32%)
  waiting for transfers between devices  295 us (20%)
  local copies, waits for them, and re-layouts  207 us (14%)
  matrix products  207 us (14%)
  other arithmetic  163 us (11%)
  starting transfers between devices  82.8 us (6%)
  between operations  19.7 us (1%)
    psum x9, blocking collectives, fine_sums(): return lax.psum(parts, ('wide', 'narrow'))  373 us
    unnamed x3, waiting for transfers between devices  229 us
    dot_general x216, matrix products, apply_taps(): jnp.dot(tap_window(padded, tap_id, extent), kernel[tap_id], preferred_ele...  124 us
    all_gather x1, other arithmetic, on_device(): lax.all_gather(params.astype(jnp.bfloat16), ('wide', 'narrow'), axis=0, t...  121 us
    concatenate x1, local copies, waits for them, and re-layouts, on_device(): jnp.concatenate([member.reshape(-1) for member in ordered] + [jnp.zeros((...  116 us
    ppermute x16, starting transfers between devices, extended(): lax.ppermute(tail, axis, [(i, (i + 1) % count) for i in range(ends)])  62 us
    dot_general x135, matrix products, kernel_grad(): lax.dot_general(tap_window(padded, tap_id, extent), flat_grad, (((0,), (0...  61.8 us
    all_gather x1, waiting for transfers between devices, on_device(): lax.all_gather(params.astype(jnp.bfloat16), ('wide', 'narrow'), axis=0, t...  61.7 us
  transfers between devices with their start and end apart: 34, of which 9 were waited for; matrix products, arithmetic and copies ran while one was open for 7% of the time, Pallas kernels for 0%

commit v1 on v0

v1 whole, which is shorter than its diff:
```python
import functools

import jax
import jax.numpy as jnp
from jax import lax
from jax.experimental import pallas as pl
from jax.experimental.pallas import tpu as pltpu
from jax.sharding import PartitionSpec as P

C1 = 128
C2 = 256
GATE = 64
CLASSES = 3
STEP = 10

EPS_NORM = 1e-05
BETA_ONE = 0.9
BETA_TWO = 0.999
EPS_ADAM = 1e-06
DECAY_RATE = 0.01
LEARN_RATE = 0.3

F32 = jnp.float32
BF16 = jnp.bfloat16
MESH = pl.DeviceIdType.MESH
LANES = 128
TILE = 16 * LANES

LENGTHS = (
    27 * C1,
    27 * C1 * C1,
    27 * C1 * C2,
    C1 * GATE,
    C2 * GATE,
    GATE,
    27 * (C1 + C2) * C1,
    27 * C1 * C1,
    (C1 + 1) * CLASSES,
    4 * C1 + C2,
    4 * C1 + C2,
)
STARTS = tuple(sum(LENGTHS[:i]) for i in range(len(LENGTHS)))
USED = sum(LENGTHS)

FRONT = 32 * LANES - STARTS[1]
SPLIT = STARTS[6]
ROW_IN = STARTS[0] + FRONT
ROW_IN = ROW_IN // LANES
ROW_ENC = (STARTS[1] + FRONT) // LANES
ROW_MID = (STARTS[2] + FRONT) // LANES
ROW_X = (STARTS[3] + FRONT) // LANES
ROW_G = (STARTS[4] + FRONT) // LANES
ROW_PSI = (STARTS[5] + FRONT) // LANES
ROWS_A = -(-(SPLIT + FRONT) // TILE) * 16
ROW_DEC1 = ROWS_A
ROW_DEC2 = ROW_DEC1 + (STARTS[7] - SPLIT) // LANES
ROW_TAIL = ROW_DEC1 + (STARTS[8] - SPLIT) // LANES

DIRS = tuple((dx, dy) for dx in (-1, 0, 1) for dy in (-1, 0, 1) if (dx, dy) != (0, 0))

N_AR = 10
N_HALO = 9


def dot(a, b):
    return jnp.dot(a, b, preferred_element_type=F32)


def dot_nt(a, b):
    return lax.dot_general(a, b, (((1,), (1,)), ((), ())), preferred_element_type=F32)


def dot_tn(a, b):
    return lax.dot_general(a, b, (((0,), (0,)), ((), ())), preferred_element_type=F32)


def iota(shape, dim):
    return lax.broadcasted_iota(jnp.int32, shape, dim)


def onehot(cond):
    return jnp.where(cond, 1.0, 0.0).astype(BF16)


def silu_grad(v, s):
    return s * (1.0 + v * (1.0 - s))


def step_kernel(cfg, ct_ref, lab_ref, val_ref, w_ref, g_ref, out_ref, *scr):
    names = cfg["names"]
    s = dict(zip(names, scr))
    nw, nn = cfg["nw"], cfg["nn"]
    total = nw * nn
    X, Y, Z = cfg["ext"]
    XE, YE = X + 2, Y + 2
    CX, CY, CZ = X // 2, Y // 2, Z // 2
    V = X * Y * Z
    VC = CX * CY * CZ
    voxels = float(V * total)
    coarse_voxels = voxels / 8.0
    w = lax.axis_index("wide")
    n = lax.axis_index("narrow")
    me = w * nn + n

    def dev(p):
        return (p // nn, lax.rem(p, nn))

    barrier = pltpu.get_barrier_semaphore()

    def greet(d, carry):
        pl.semaphore_signal(
            barrier, inc=1, device_id=dev(lax.rem(me + d, total)), device_id_type=MESH
        )
        return carry

    lax.fori_loop(1, total, greet, 0)
    pl.semaphore_wait(barrier, total - 1)

    slots, ar_send, ar_recv = s["slots"], s["ar_send"], s["ar_recv"]

    def ar_start(r, rows):
        rows = list(rows) + [jnp.zeros((1, LANES), F32)] * (4 - len(rows))
        slots[r, me] = jnp.concatenate(rows, 0)

        def push(d, carry):
            pltpu.make_async_remote_copy(
                slots.at[r, me],
                slots.at[r, me],
                ar_send.at[r],
                ar_recv.at[r],
                device_id=dev(lax.rem(me + d, total)),
                device_id_type=MESH,
            ).start()
            return carry

        lax.fori_loop(1, total, push, 0)

    def ar_whole(r):
        others = slots.at[r, pl.ds(0, total - 1)]
        return pltpu.make_async_remote_copy(
            others, others, ar_send.at[r], ar_recv.at[r], device_id=(w, n), device_id_type=MESH
        )

    def ar_wait(r):
        ar_whole(r).wait_recv()
        return jnp.sum(slots[r], axis=0)

    side, side_send, side_recv = s["side"], s["side_send"], s["side_recv"]

    def side_start(rows):
        rows = list(rows) + [jnp.zeros((1, LANES), F32)] * (8 - len(rows))
        side[me] = jnp.concatenate(rows, 0)

        def push(d, carry):
            pltpu.make_async_remote_copy(
                side.at[me],
                side.at[me],
                side_send,
                side_recv,
                device_id=dev(lax.rem(me + d, total)),
                device_id_type=MESH,
            ).start()
            return carry

        lax.fori_loop(1, total, push, 0)

    def side_whole():
        others = side.at[pl.ds(0, total - 1)]
        return pltpu.make_async_remote_copy(
            others, others, side_send, side_recv, device_id=(w, n), device_id_type=MESH
        )

    halo_send, halo_recv = s["halo_send"], s["halo_recv"]

    def halo_copy(h, ref, i):
        dx, dy = DIRS[i]
        ex, ey = ref.shape[0] - 2, ref.shape[1] - 2

        def source(d, size):
            return pl.ds(1, size) if d == 0 else pl.ds(size if d > 0 else 1, 1)

        def target(d, size):
            return pl.ds(1, size) if d == 0 else pl.ds(0 if d > 0 else size + 1, 1)

        return pltpu.make_async_remote_copy(
            ref.at[source(dx, ex), source(dy, ey)],
            ref.at[target(dx, ex), target(dy, ey)],
            halo_send.at[h, i],
            halo_recv.at[h, i],
            device_id=(lax.rem(w + dx + nw, nw), lax.rem(n + dy + nn, nn)),
            device_id_type=MESH,
        )

    def halo_start(h, ref):
        for i in range(8):
            halo_copy(h, ref, i).start()

    def halo_wait(h, ref):
        for i in range(8):
            halo_copy(h, ref, i).wait_recv()

    def clear_edges(ref, depth):
        ex, ey = ref.shape[0], ref.shape[1]

        @pl.when(w == 0)
        def _():
            ref[0:depth] = jnp.zeros((depth,) + ref.shape[1:], ref.dtype)

        @pl.when(w == nw - 1)
        def _():
            ref[ex - depth : ex] = jnp.zeros((depth,) + ref.shape[1:], ref.dtype)

        @pl.when(n == 0)
        def _():
            ref[:, 0:depth] = jnp.zeros((ex, depth) + ref.shape[2:], ref.dtype)

        @pl.when(n == nn - 1)
        def _():
            ref[:, ey - depth : ey] = jnp.zeros((ex, depth) + ref.shape[2:], ref.dtype)

    def z_three(flat, length):
        rows = flat.shape[0]
        at = jnp.bitwise_and(iota(flat.shape, 0), length - 1)
        before = jnp.where(at == 0, 0.0, pltpu.roll(flat, 1, 0))
        after = jnp.where(at == length - 1, 0.0, pltpu.roll(flat, rows - 1, 0))
        return before.astype(BF16), flat.astype(BF16), after.astype(BF16)

    def put_three(ref, flat, base, stride):
        shape = ref.shape[:3] + (LANES,)
        for c, part in enumerate(z_three(flat, ref.shape[2])):
            lo = c * stride + base
            ref[:, :, :, lo : lo + LANES] = part.reshape(shape)

    def merge_frame(full, low):
        ex, ey = full.shape[0], full.shape[1]
        full[0] = low[0].astype(F32)
        full[ex - 1] = low[ex - 1].astype(F32)
        full[1 : ex - 1, 0] = low[1 : ex - 1, 0].astype(F32)
        full[1 : ex - 1, ey - 1] = low[1 : ex - 1, ey - 1].astype(F32)

    def conv(ref, weight, row0, ext):
        x, y = ext
        rows = x * y * ref.shape[2]
        depth = ref.shape[3]
        acc = None
        for ab in range(9):
            a, b = ab // 3, ab % 3
            window = ref[a : a + x, b : b + y].reshape(rows, depth)
            part = dot(window, weight[row0 + ab * depth : row0 + (ab + 1) * depth, :])
            acc = part if acc is None else acc + part
        return acc

    def conv_back(ref, weight, row0, cin, cout, ext):
        x, y = ext
        rows = x * y * ref.shape[2]
        acc = None
        for ab in range(9):
            a, b = ab // 3, ab % 3
            for c in range(3):
                window = ref[a : a + x, b : b + y, :, c * cout : (c + 1) * cout]
                tap = 26 - (3 * ab + c)
                part = dot_nt(
                    window.reshape(rows, cout),
                    weight[row0 + tap * cin : row0 + (tap + 1) * cin, :],
                )
                acc = part if acc is None else acc + part
        return acc

    def conv_grad(ref, low, row0, ext):
        x, y = ext
        rows = x * y * ref.shape[2]
        depth = ref.shape[3]
        for ab in range(9):
            a, b = ab // 3, ab % 3
            window = ref[a : a + x, b : b + y].reshape(rows, depth)
            g_ref[row0 + ab * depth : row0 + (ab + 1) * depth, :] = dot_tn(window, low).astype(BF16)

    def col_sum(v):
        return jnp.sum(v, axis=0, keepdims=True)

    def own(ref):
        return ref[1 : ref.shape[0] - 1, 1 : ref.shape[1] - 1]

    def flat(v):
        return v.reshape(-1, v.shape[-1])

    pair = s["pair"]

    def pool(v):
        v = v.reshape(X, Y, Z, LANES)
        v = v[0] + v[1]
        v = v.reshape(CY, 2, Z, LANES)
        v = v[:, 0] + v[:, 1]
        pair[0 : CY * Z] = v.reshape(CY * Z, LANES)
        return pair[pl.ds(0, VC, stride=2), :] + pair[pl.ds(1, VC, stride=2), :]

    def spread(v):
        pair[pl.ds(0, VC, stride=2), :] = v
        pair[pl.ds(1, VC, stride=2), :] = v
        u = pair[0 : CY * Z].reshape(CY, 1, Z, LANES)
        u = jnp.broadcast_to(u, (CY, 2, Z, LANES)).reshape(1, Y, Z, LANES)
        return jnp.broadcast_to(u, (X, Y, Z, LANES)).reshape(V, LANES)

    def stats(total_rows, count):
        half = total_rows.shape[0] // 2
        parts = [total_rows[i : i + 1] for i in range(2 * half)]
        mean = jnp.concatenate(parts[:half], 1) / count
        spread_v = jnp.concatenate(parts[half:], 1) / count - mean * mean
        return mean, lax.rsqrt(spread_v + EPS_NORM)

    cts, ct_send, ct_recv = s["cts"], s["ct_send"], s["ct_recv"]
    cts[4] = ct_ref[...]

    def ct_copy(i):
        dx, dy = DIRS[i]
        return pltpu.make_async_remote_copy(
            cts.at[4],
            cts.at[3 * (1 - dx) + 1 - dy],
            ct_send.at[i],
            ct_recv.at[i],
            device_id=(lax.rem(w + dx + nw, nw), lax.rem(n + dy + nn, nn)),
            device_id_type=MESH,
        )

    for i in range(8):
        ct_copy(i).start()

    tail = w_ref[ROW_TAIL : ROW_TAIL + 16, :].astype(F32)
    used_rows = CLASSES * (C1 + 1) // LANES
    used_lanes = CLASSES * (C1 + 1) % LANES
    rolled = pltpu.roll(tail, LANES - used_lanes, 1)
    lane_id = iota((1, LANES), 1)

    def tail_row(q):
        r = used_rows + q
        return jnp.where(
            lane_id < LANES - used_lanes, rolled[r : r + 1], rolled[r + 1 : r + 2]
        )

    gains = [tail_row(q) for q in range(6)]
    shifts = [tail_row(6 + q) for q in range(6)]
    gain = [gains[0], gains[1], jnp.concatenate(gains[2:4], 1), gains[4], gains[5]]
    shift = [shifts[0], shifts[1], jnp.concatenate(shifts[2:4], 1), shifts[4], shifts[5]]

    def select_head(j, r):
        return onehot(
            LANES * r + iota((LANES, LANES), 0) == CLASSES * iota((LANES, LANES), 1) + j
        )

    tail_low = tail.astype(BF16)
    head_rows = []
    for j in range(CLASSES):
        row = None
        for r in range(CLASSES):
            part = dot(tail_low, select_head(j, r))[r : r + 1]
            row = part if row is None else row + part
        head_rows.append(row)
    head_t = jnp.concatenate(head_rows + [jnp.zeros((8 - CLASSES, LANES), F32)], 0).astype(BF16)
    bias_row = tail[used_rows : used_rows + 1]
    bias_col = jnp.sum(
        jnp.where(iota((8, LANES), 0) == iota((8, LANES), 1), bias_row, 0.0), axis=1, keepdims=True
    )
    bias_col = jnp.where(iota((8, 1), 0) < CLASSES, bias_col, 0.0)
    psi = w_ref[ROW_PSI : ROW_PSI + 16, :].astype(F32)[0:1]
    psi = jnp.where(lane_id < GATE, psi, 0.0)

    def pick_half(h, rows):
        return onehot(iota((2 * rows, rows), 0) == 2 * iota((2 * rows, rows), 1) + h)

    def widen(block, rows):
        block = block.astype(F32)
        lower = jnp.where(lane_id < GATE, block, 0.0).astype(BF16)
        upper = jnp.where(lane_id < GATE, pltpu.roll(block, GATE, 1), 0.0).astype(BF16)
        both = dot(pick_half(0, rows), lower) + dot(pick_half(1, rows), upper)
        return both.astype(BF16)

    def narrow_back(block, rows):
        low = block.astype(BF16)
        lower = dot_tn(pick_half(0, rows), low)
        upper = dot_tn(pick_half(1, rows), low)
        return (lower + pltpu.roll(upper, GATE, 1)).astype(BF16)

    w_x = widen(w_ref[ROW_X : ROW_X + C1 // 2, :], C1 // 2)
    w_g = widen(w_ref[ROW_G : ROW_G + C2 // 2, :], C2 // 2)

    front = w_ref[0:32, :].astype(F32)
    we = s["we"]
    for ab in range(9):
        taps = [
            jnp.broadcast_to(front[ROW_IN + 3 * ab + c : ROW_IN + 3 * ab + c + 1], (Z, LANES))
            for c in range(3)
        ]
        taps.append(jnp.zeros((LANES - 3 * Z, LANES), F32))
        we[ab * LANES : (ab + 1) * LANES] = jnp.concatenate(taps, 0).astype(BF16)

    shuffle = onehot(
        iota((C2, C2), 1)
        == jnp.bitwise_and(iota((C2, C2), 0), 1) * C1 + lax.shift_right_logical(iota((C2, C2), 0), 1)
    )
    wm = s["wm"]
    for tap in range(27):
        part = dot_tn(shuffle, w_ref[ROW_MID + C2 * tap : ROW_MID + C2 * (tap + 1), :]).astype(BF16)
        wm[tap * C1 : (tap + 1) * C1, 0:LANES] = part[0:LANES]
        wm[tap * C1 : (tap + 1) * C1, LANES:C2] = part[LANES:C2]

    valid = val_ref[...]
    count_row = jnp.broadcast_to(jnp.sum(valid, axis=1, keepdims=True), (1, LANES))

    for i in range(8):
        ct_copy(i).wait_recv()

    entry = s["entry"]
    zz, ll = iota((Z, LANES), 0), iota((Z, LANES), 1)
    band = jnp.where((jnp.bitwise_and(ll, Z - 1) == zz + ll // Z - 1) & (ll < 3 * Z), 1.0, 0.0)
    for ex in range(X + 4):
        bx = (ex - 2 + X) // X
        lx = ex - 2 - (bx - 1) * X
        for ey in range(Y + 4):
            by = (ey - 2 + Y) // Y
            ly = ey - 2 - (by - 1) * Y
            row = cts[3 * bx + by, lx * Y + ly : lx * Y + ly + 1]
            entry[ex, ey] = (jnp.broadcast_to(row, (Z, LANES)) * band).astype(BF16)
    clear_edges(entry, 2)
    raw1 = s["raw1"]
    raw1[...] = conv(entry, we, 0, (XE, YE)).reshape(XE, YE, Z, LANES)
    mine = flat(own(raw1))
    ar_start(0, [col_sum(mine), col_sum(mine * mine), count_row])
    sums = ar_wait(0)
    valid_count = sums[2:3, 0:1]
    mean1, inv1 = stats(sums[0:2], voxels)
    v = (flat(raw1[...]) - mean1) * inv1 * gain[0] + shift[0]
    pad1 = s["pad1"]
    put_three(pad1, v * jax.nn.sigmoid(v), 0, C1)
    clear_edges(pad1, 1)

    raw2, low2 = s["raw2"], s["low2"]
    mine = conv(pad1, w_ref, ROW_ENC, (X, Y))
    raw2[1 : XE - 1, 1 : YE - 1] = mine.reshape(X, Y, Z, C1)
    low2[1 : XE - 1, 1 : YE - 1] = mine.astype(BF16).reshape(X, Y, Z, C1)
    ar_start(1, [col_sum(mine), col_sum(mine * mine)])
    halo_start(0, low2)
    sums = ar_wait(1)
    mean2, inv2 = stats(sums[0:2], voxels)
    v = (mine - mean2) * inv2 * gain[1] + shift[1]
    skip_own = v * jax.nn.sigmoid(v)

    pool_in = s["pool_in"]
    pool_in[1 : CX + 1, 1 : CY + 1] = (pool(skip_own) * 0.125).astype(BF16).reshape(CX, CY, CZ, C1)
    halo_start(1, pool_in)
    halo_wait(0, low2)
    merge_frame(raw2, low2)
    v = (flat(raw2[...]) - mean2) * inv2 * gain[1] + shift[1]
    skip = s["skip"]
    skip_all = v * jax.nn.sigmoid(v)
    skip[...] = skip_all.reshape(XE, YE, Z, C1)
    mix = s["mix"]
    mix[...] = dot(skip_all.astype(BF16), w_x).reshape(XE, YE, Z, LANES)
    halo_wait(1, pool_in)
    clear_edges(pool_in, 1)
    pad_mid = s["pad_mid"]
    put_three(pad_mid, flat(pool_in[...].astype(F32)), 0, C1)
    raw3, low3 = s["raw3"], s["low3"]
    mine = conv(pad_mid, wm, 0, (CX, CY))
    raw3[1 : CX + 1, 1 : CY + 1] = mine.reshape(CX, CY, CZ, C2)
    low3[1 : CX + 1, 1 : CY + 1] = mine.astype(BF16).reshape(CX, CY, CZ, C2)
    sum_v, square_v = col_sum(mine), col_sum(mine * mine)
    ar_start(
        2, [sum_v[:, 0:C1], sum_v[:, C1:C2], square_v[:, 0:C1], square_v[:, C1:C2]]
    )
    halo_start(2, low3)
    sums = ar_wait(2)
    mean3, inv3 = stats(sums, coarse_voxels)
    halo_wait(2, low3)
    merge_frame(raw3, low3)
    v = (flat(raw3[...]) - mean3) * inv3 * gain[2] + shift[2]
    coarse = (v * jax.nn.sigmoid(v)).astype(BF16).reshape(CX + 2, CY + 2, CZ, C2)
    coarse_own = flat(coarse[1 : CX + 1, 1 : CY + 1])
    frame = (CY + 2) * CZ
    doubled = onehot(
        iota((2 * frame, frame), 1) == lax.shift_right_logical(iota((2 * frame, frame), 0), 1)
    )
    tall = s["tall"]
    for cx in range(CX + 2):
        tall[cx] = (
            dot(doubled, coarse[cx].reshape(frame, C2)).astype(BF16).reshape(CY + 2, Z, C2)
        )

    def expand(u):
        u = jnp.concatenate([u[(i + 1) // 2 : (i + 1) // 2 + 1] for i in range(XE)], 0)
        return jnp.concatenate([u[:, (j + 1) // 2 : (j + 1) // 2 + 1] for j in range(YE)], 1)

    gate_c = dot(flat(tall[...]), w_g).reshape(CX + 2, CY + 2, Z, LANES)
    mixed_in = flat(mix[...] + expand(gate_c))
    mix[...] = mixed_in.reshape(XE, YE, Z, LANES)
    mixed = mixed_in * jax.nn.sigmoid(mixed_in)
    att = jax.nn.sigmoid(jnp.sum(mixed * psi, axis=1, keepdims=True))
    attention = s["attention"]
    attention[...] = jnp.broadcast_to(att, (XE * YE * Z, LANES)).reshape(XE, YE, Z, LANES)
    pad_join = s["pad_join"]
    put_three(pad_join, flat(skip[...] * attention[...]), 0, C1 + C2)
    for half in range(2):
        piece = flat(tall[:, :, :, half * C1 : (half + 1) * C1].astype(F32))
        for c, part in enumerate(z_three(piece, Z)):
            lo = c * (C1 + C2) + C1 + half * C1
            pad_join[:, :, :, lo : lo + C1] = expand(part.reshape(CX + 2, CY + 2, Z, C1))
    clear_edges(pad_join, 1)

    raw4, low4 = s["raw4"], s["low4"]
    mine = conv(pad_join, w_ref, ROW_DEC1, (X, Y))
    raw4[1 : XE - 1, 1 : YE - 1] = mine.reshape(X, Y, Z, C1)
    low4[1 : XE - 1, 1 : YE - 1] = mine.astype(BF16).reshape(X, Y, Z, C1)
    ar_start(3, [col_sum(mine), col_sum(mine * mine)])
    halo_start(3, low4)
    sums = ar_wait(3)
    mean4, inv4 = stats(sums[0:2], voxels)
    halo_wait(3, low4)
    merge_frame(raw4, low4)
    v = (flat(raw4[...]) - mean4) * inv4 * gain[3] + shift[3]
    pad4 = s["pad4"]
    put_three(pad4, v * jax.nn.sigmoid(v), 0, C1)
    clear_edges(pad4, 1)

    raw5, low5 = s["raw5"], s["low5"]
    mine = conv(pad4, w_ref, ROW_DEC2, (X, Y))
    raw5[1 : XE - 1, 1 : YE - 1] = mine.reshape(X, Y, Z, C1)
    low5[1 : XE - 1, 1 : YE - 1] = mine.astype(BF16).reshape(X, Y, Z, C1)
    ar_start(4, [col_sum(mine), col_sum(mine * mine)])
    halo_start(4, low5)
    sums = ar_wait(4)
    mean5, inv5 = stats(sums[0:2], voxels)
    hat = (mine - mean5) * inv5
    v = hat * gain[4] + shift[4]
    sg = jax.nn.sigmoid(v)
    act = (v * sg).astype(BF16)

    logits = dot_nt(head_t, act) + bias_col
    real = iota((8, V), 0) < CLASSES
    logits = jnp.where(real, logits, -1e30)
    hot = iota((8, V), 0) == lab_ref[...]
    top = jnp.max(logits, axis=0, keepdims=True)
    log_total = top + jnp.log(jnp.sum(jnp.exp(logits - top), axis=0, keepdims=True))
    picked = jnp.sum(jnp.where(hot, logits, 0.0), axis=0, keepdims=True)
    loss = jnp.sum(valid * (log_total - picked), axis=1, keepdims=True)
    probs = jnp.exp(logits - log_total)
    g_logits = valid * (probs - jnp.where(hot, 1.0, 0.0)) / valid_count
    g_low = g_logits.astype(BF16)
    head_grad = dot(g_low, act)
    bias_grad = jnp.sum(g_low.astype(F32), axis=1, keepdims=True)
    bias_line = jnp.sum(
        jnp.where(iota((8, LANES), 0) == iota((8, LANES), 1), bias_grad, 0.0), axis=0, keepdims=True
    )
    dy = dot_tn(g_low, head_t) * silu_grad(v, sg)

    def norm_back(r, h, dy, hat, raw, mean, inv, gain_v, ext, count, names2, extra):
        dyf, dyl = s[names2[0]], s[names2[1]]
        ex, ey = ext[0] + 2, ext[1] + 2
        width = dy.shape[1]
        shaped = dy.reshape(ext + (width,))
        dyf[1 : ex - 1, 1 : ey - 1] = shaped
        dyl[1 : ex - 1, 1 : ey - 1] = shaped.astype(BF16)
        first, second = col_sum(dy), col_sum(dy * hat)
        rows = [first[:, i : i + LANES] for i in range(0, width, LANES)]
        rows += [second[:, i : i + LANES] for i in range(0, width, LANES)]
        ar_start(r, rows + extra)
        halo_start(h, dyl)
        return rows

    def norm_back_end(r, h, raw, mean, inv, gain_v, count, names2):
        dyf, dyl = s[names2[0]], s[names2[1]]
        sums = ar_wait(r)
        halo_wait(h, dyl)
        merge_frame(dyf, dyl)
        width = dyf.shape[3]
        k = width // LANES
        one = jnp.concatenate([sums[i : i + 1] for i in range(k)], 1)
        two = jnp.concatenate([sums[k + i : k + i + 1] for i in range(k)], 1)
        hat_all = (flat(raw[...]) - mean) * inv
        back = inv * gain_v * (flat(dyf[...]) - one / count - hat_all * (two / count))
        return sums, back

    grad_shift, grad_gain = {}, {}
    fine = (X, Y, Z)
    norm_back(5, 5, dy, hat, raw5, mean5, inv5, gain[4], fine, voxels, ("dy5", "dyl5"),
              [jnp.broadcast_to(loss, (1, LANES))])
    halo_wait(4, low5)
    merge_frame(raw5, low5)
    sums, back = norm_back_end(5, 5, raw5, mean5, inv5, gain[4], voxels, ("dy5", "dyl5"))
    grad_shift[4], grad_gain[4] = [sums[0:1]], [sums[1:2]]
    loss_row = sums[2:3]
    dpad = s["dpad5"]
    put_three(dpad, back, 0, C1)
    clear_edges(dpad, 1)
    grad_act = conv_back(dpad, w_ref, ROW_DEC2, C1, C1, (X, Y))
    hat = (flat(own(raw4)) - mean4) * inv4
    v = hat * gain[3] + shift[3]
    dy = grad_act * silu_grad(v, jax.nn.sigmoid(v))
    norm_back(6, 6, dy, hat, raw4, mean4, inv4, gain[3], fine, voxels, ("dy4", "dyl4"), [])
    conv_grad(pad4, flat(own(dpad)[:, :, :, C1 : 2 * C1]), ROW_DEC2, (X, Y))
    sums, back = norm_back_end(6, 6, raw4, mean4, inv4, gain[3], voxels, ("dy4", "dyl4"))
    grad_shift[3], grad_gain[3] = [sums[0:1]], [sums[1:2]]
    dpad = s["dpad4"]
    put_three(dpad, back, 0, C1)
    clear_edges(dpad, 1)
    low_raw4 = flat(own(dpad)[:, :, :, C1 : 2 * C1])
    grad_join = conv_back(dpad, w_ref, ROW_DEC1, C1 + C2, C1, (X, Y))

    grad_gated = grad_join[:, 0:C1]
    skip_own = flat(own(skip))
    att_own = flat(own(attention))
    mixed_own = flat(own(mix))
    sg = jax.nn.sigmoid(mixed_own)
    d_att = jnp.sum(grad_gated * skip_own, axis=1, keepdims=True)
    d_logit = d_att * att_own * (1.0 - att_own)
    psi_grad = col_sum(mixed_own * sg * d_logit)
    d_mixed = d_logit * psi * silu_grad(mixed_own, sg)
    low_fine = d_mixed.astype(BF16)
    low_gc = pool(d_mixed).astype(BF16)
    d_coarse = [
        pool(grad_join[:, C1 : 2 * C1]),
        pool(grad_join[:, 2 * C1 : 3 * C1]),
    ]
    d_coarse = jnp.concatenate(d_coarse, 1) + dot_nt(low_gc, w_g)
    d_coarse = d_coarse.astype(BF16).astype(F32)
    hat = (flat(own(raw3)) - mean3) * inv3
    v = hat * gain[2] + shift[2]
    dy = d_coarse * silu_grad(v, jax.nn.sigmoid(v))
    norm_back(7, 7, dy, hat, raw3, mean3, inv3, gain[2], (CX, CY, CZ), coarse_voxels, ("dy3", "dyl3"), [])
    side_start([head_grad[0:1], head_grad[1:2], head_grad[2:3], bias_line, psi_grad])
    d_skip = s["d_skip"]
    d_skip[...] = grad_gated * att_own + dot_nt(low_fine, w_x)
    conv_grad(pad_join, low_raw4, ROW_DEC1, (X, Y))
    g_ref[ROW_X : ROW_X + C1 // 2, :] = narrow_back(
        dot_tn(skip_own.astype(BF16), low_fine), C1 // 2
    )
    g_ref[ROW_G : ROW_G + C2 // 2, :] = narrow_back(dot_tn(coarse_own, low_gc), C2 // 2)
    sums, back = norm_back_end(7, 7, raw3, mean3, inv3, gain[2], coarse_voxels, ("dy3", "dyl3"))
    grad_shift[2], grad_gain[2] = [sums[0:1], sums[1:2]], [sums[2:3], sums[3:4]]
    dpad = s["dpad3"]
    put_three(dpad, back[:, 0:C1], 0, C2)
    put_three(dpad, back[:, C1:C2], C1, C2)
    clear_edges(dpad, 1)
    low_raw3 = flat(own(dpad)[:, :, :, C2 : 2 * C2])
    d_pool = conv_back(dpad, wm, 0, C1, C2, (CX, CY))
    grad_skip = d_skip[...] + spread(d_pool) * 0.125
    hat = (flat(own(raw2)) - mean2) * inv2
    v = hat * gain[1] + shift[1]
    dy = grad_skip * silu_grad(v, jax.nn.sigmoid(v))
    norm_back(8, 8, dy, hat, raw2, mean2, inv2, gain[1], fine, voxels, ("dy2", "dyl2"), [])
    for ab in range(9):
        window = pad_mid[ab // 3 : ab // 3 + CX, ab % 3 : ab % 3 + CY].reshape(VC, 3 * C1)
        block = dot_tn(window, low_raw3).astype(BF16)
        for c in range(3):
            stacked = block[c * C1 : (c + 1) * C1]
            stacked = jnp.concatenate([stacked[:, 0:C1], stacked[:, C1:C2]], 0)
            lo = ROW_MID + (3 * ab + c) * C2
            g_ref[lo : lo + C2, :] = dot(shuffle, stacked).astype(BF16)
    sums, back = norm_back_end(8, 8, raw2, mean2, inv2, gain[1], voxels, ("dy2", "dyl2"))
    grad_shift[1], grad_gain[1] = [sums[0:1]], [sums[1:2]]
    dpad = s["dpad2"]
    put_three(dpad, back, 0, C1)
    clear_edges(dpad, 1)
    low_raw2 = flat(own(dpad)[:, :, :, C1 : 2 * C1])
    grad_act = conv_back(dpad, w_ref, ROW_ENC, C1, C1, (X, Y))
    hat1 = (flat(own(raw1)) - mean1) * inv1
    v = hat1 * gain[0] + shift[0]
    dy = grad_act * silu_grad(v, jax.nn.sigmoid(v))
    ar_start(9, [col_sum(dy), col_sum(dy * hat1)])
    conv_grad(pad1, low_raw2, ROW_ENC, (X, Y))
    sums = ar_wait(9)
    grad_shift[0], grad_gain[0] = [sums[0:1]], [sums[1:2]]
    back = inv1 * gain[0] * (dy - sums[0:1] / voxels - hat1 * (sums[1:2] / voxels))
    low_raw1 = back.astype(BF16)
    in_rows = []
    for ab in range(9):
        a, b = ab // 3, ab % 3
        window = entry[a + 1 : a + 1 + X, b + 1 : b + 1 + Y].reshape(V, LANES)
        block = dot_tn(window, low_raw1)
        for c in range(3):
            in_rows.append(col_sum(block[c * Z : (c + 1) * Z]))
    in_rows = [jnp.zeros((ROW_IN, LANES), F32)] + in_rows
    g_ref[0:32, :] = jnp.concatenate(in_rows, 0).astype(BF16)

    side_whole().wait_recv()
    small = jnp.sum(side[...], axis=0)
    flat_rows = []
    for r in range(CLASSES):
        row = None
        for j in range(CLASSES):
            part = lax.dot_general(
                small,
                select_head(j, r).astype(F32),
                (((1,), (1,)), ((), ())),
                preferred_element_type=F32,
                precision=lax.Precision.HIGHEST,
            )[j : j + 1]
            row = part if row is None else row + part
        flat_rows.append(row)
    later = []
    for group in (grad_gain, grad_shift):
        for layer in range(5):
            later += group[layer]
    later = [pltpu.roll(row, used_lanes, 1) for row in later]
    flat_rows.append(jnp.where(lane_id < used_lanes, small[3:4], later[0]))
    for q in range(1, 12):
        flat_rows.append(jnp.where(lane_id < used_lanes, later[q - 1], later[q]))
    flat_rows.append(jnp.where(lane_id < used_lanes, later[11], 0.0))
    out_ref[0:16] = jnp.concatenate(flat_rows, 0)
    out_ref[16:24] = jnp.concatenate(
        [
            jnp.where(lane_id < GATE, small[4:5], 0.0),
            loss_row,
            jnp.broadcast_to(valid_count, (1, LANES)),
            jnp.zeros((5, LANES), F32),
        ],
        0,
    )

    for r in range(N_AR):
        ar_whole(r).wait_send()
    side_whole().wait_send()
    for i in range(8):
        ct_copy(i).wait_send()
    for h, name in enumerate(
        ("low2", "pool_in", "low3", "low4", "low5", "dyl5", "dyl4", "dyl3", "dyl2")
    ):
        for i in range(8):
            halo_copy(h, s[name], i).wait_send()


def step_call(nw, nn, ext, ct, lab, val, weights):
    X, Y, Z = ext
    XE, YE = X + 2, Y + 2
    CX, CY, CZ = X // 2, Y // 2, Z // 2
    total = nw * nn
    framed = (XE, YE, Z)
    small = (CX + 2, CY + 2, CZ)
    dma = pltpu.SemaphoreType.DMA
    scratch = {
        "slots": pltpu.VMEM((N_AR, total, 4, LANES), F32),
        "ar_send": dma((N_AR,)),
        "ar_recv": dma((N_AR,)),
        "side": pltpu.VMEM((total, 8, LANES), F32),
        "side_send": dma,
        "side_recv": dma,
        "halo_send": dma((N_HALO, 8)),
        "halo_recv": dma((N_HALO, 8)),
        "cts": pltpu.VMEM((9, X * Y, LANES), F32),
        "ct_send": dma((8,)),
        "ct_recv": dma((8,)),
        "pair": pltpu.VMEM((CY * Z, LANES), F32),
        "we": pltpu.VMEM((9 * LANES, LANES), BF16),
        "wm": pltpu.VMEM((27 * C1, C2), BF16),
        "entry": pltpu.VMEM((X + 4, Y + 4, Z, LANES), BF16),
        "raw1": pltpu.VMEM(framed + (C1,), F32),
        "pad1": pltpu.VMEM(framed + (3 * C1,), BF16),
        "raw2": pltpu.VMEM(framed + (C1,), F32),
        "low2": pltpu.VMEM(framed + (C1,), BF16),
        "pool_in": pltpu.VMEM(small + (C1,), BF16),
        "skip": pltpu.VMEM(framed + (C1,), F32),
        "mix": pltpu.VMEM(framed + (LANES,), F32),
        "attention": pltpu.VMEM(framed + (LANES,), F32),
        "pad_mid": pltpu.VMEM(small + (3 * C1,), BF16),
        "raw3": pltpu.VMEM(small + (C2,), F32),
        "low3": pltpu.VMEM(small + (C2,), BF16),
        "tall": pltpu.VMEM((CX + 2, CY + 2, Z, C2), BF16),
        "pad_join": pltpu.VMEM(framed + (3 * (C1 + C2),), BF16),
        "raw4": pltpu.VMEM(framed + (C1,), F32),
        "low4": pltpu.VMEM(framed + (C1,), BF16),
        "pad4": pltpu.VMEM(framed + (3 * C1,), BF16),
        "raw5": pltpu.VMEM(framed + (C1,), F32),
        "low5": pltpu.VMEM(framed + (C1,), BF16),
        "dy5": pltpu.VMEM(framed + (C1,), F32),
        "dyl5": pltpu.VMEM(framed + (C1,), BF16),
        "dpad5": pltpu.VMEM(framed + (3 * C1,), BF16),
        "dy4": pltpu.VMEM(framed + (C1,), F32),
        "dyl4": pltpu.VMEM(framed + (C1,), BF16),
        "dpad4": pltpu.VMEM(framed + (3 * C1,), BF16),
        "dy3": pltpu.VMEM(small + (C2,), F32),
        "dyl3": pltpu.VMEM(small + (C2,), BF16),
        "dpad3": pltpu.VMEM(small + (3 * C2,), BF16),
        "dy2": pltpu.VMEM(framed + (C1,), F32),
        "dyl2": pltpu.VMEM(framed + (C1,), BF16),
        "dpad2": pltpu.VMEM(framed + (3 * C1,), BF16),
        "d_skip": pltpu.VMEM((X * Y * Z, C1), F32),
    }
    cfg = {"nw": nw, "nn": nn, "ext": ext, "names": tuple(scratch)}
    vmem = pl.BlockSpec(memory_space=pltpu.VMEM)
    return pl.pallas_call(
        functools.partial(step_kernel, cfg),
        out_shape=(
            jax.ShapeDtypeStruct(weights.shape, BF16),
            jax.ShapeDtypeStruct((24, LANES), F32),
        ),
        in_specs=[vmem] * 4,
        out_specs=(vmem, vmem),
        scratch_shapes=list(scratch.values()),
        compiler_params=pltpu.CompilerParams(
            collective_id=0, has_side_effects=True, vmem_limit_bytes=60 * 1024 * 1024
        ),
    )(ct, lab, val, weights)


def on_device(params, first_moment, second_moment, ct_image, labels, valid_mask):
    shard_len = params.shape[0]
    n_wide = lax.axis_size("wide")
    n_narrow = lax.axis_size("narrow")
    devices = n_wide * n_narrow
    place = lax.axis_index(("wide", "narrow"))
    ext = ct_image.shape
    gathered = lax.all_gather(params.astype(BF16), ("wide", "narrow"), axis=0, tiled=True)
    part_a = jnp.concatenate(
        [jnp.zeros((FRONT,), BF16), gathered[: ROWS_A * LANES - FRONT]]
    ).reshape(-1, LANES)
    n_b = -(-(shard_len * devices - SPLIT) // TILE) * TILE
    part_b = jnp.concatenate(
        [gathered[SPLIT:], jnp.zeros((n_b - (shard_len * devices - SPLIT),), BF16)]
    ).reshape(-1, LANES)
    weights = jnp.concatenate([part_a, part_b], 0)
    ct = ct_image.astype(F32).reshape(-1, ext[2])
    ct = jnp.concatenate([ct, ct, ct, jnp.zeros((ct.shape[0], LANES - 3 * ext[2]), F32)], 1)
    grads, small = step_call(
        n_wide,
        n_narrow,
        ext,
        ct,
        labels.reshape(1, -1),
        valid_mask.astype(F32).reshape(1, -1),
        weights,
    )
    first = (place == 0).astype(F32)
    flat_grad = jnp.concatenate(
        [
            grads[ROW_IN:ROW_PSI].reshape(-1).astype(F32),
            small[16, :GATE] * first,
            grads[ROW_DEC1:ROW_TAIL].reshape(-1).astype(F32),
            small[0:16].reshape(-1)[: USED - STARTS[8]] * first,
            jnp.zeros((shard_len * devices - USED,), F32),
        ]
    )
    loss_sum = small[17, 0]
    valid_count = small[18, 0]
    gradient = lax.psum_scatter(flat_grad, ("wide", "narrow"), scatter_dimension=0, tiled=True)
    new_first = BETA_ONE * first_moment + (1.0 - BETA_ONE) * gradient
    new_second = BETA_TWO * second_moment + (1.0 - BETA_TWO) * gradient * gradient
    update = (
        new_first
        / (1.0 - BETA_ONE**STEP)
        / (jnp.sqrt(new_second / (1.0 - BETA_TWO**STEP)) + EPS_ADAM)
        + DECAY_RATE * params
    )
    seg_lower = jnp.array(STARTS + (USED,), jnp.int32)
    seg_upper = jnp.array(STARTS[1:] + (USED, shard_len * devices), jnp.int32)
    position = place * shard_len + lax.iota(jnp.int32, shard_len)
    member_map = (
        (position[:, None] >= seg_lower[None]) & (position[:, None] < seg_upper[None])
    ).astype(F32)
    weight_sq = jnp.dot(params * params, member_map, precision=lax.Precision.HIGHEST)
    update_sq = jnp.dot(update * update, member_map, precision=lax.Precision.HIGHEST)
    weight_sq, update_sq = lax.psum((weight_sq, update_sq), ("wide", "narrow"))
    trust_ratio = jnp.sqrt(weight_sq) / jnp.sqrt(update_sq)
    new_params = (
        params
        - LEARN_RATE * jnp.dot(member_map, trust_ratio, precision=lax.Precision.HIGHEST) * update
    )
    return (new_params, new_first, new_second, loss_sum, valid_count)


def solution(mesh):
    in_specs = (
        P(("wide", "narrow")),
        P(("wide", "narrow")),
        P(("wide", "narrow")),
        P("wide", "narrow", None),
        P("wide", "narrow", None),
        P("wide", "narrow", None),
    )
    out_specs = (P(("wide", "narrow")), P(("wide", "narrow")), P(("wide", "narrow")), P(), P())
    return jax.shard_map(
        on_device, mesh=mesh, in_specs=in_specs, out_specs=out_specs, check_vma=False
    )
```

time: 1460 us -> 794 us (0.54)
  blocking collectives: 465 us -> 40.1 us
  matrix products: 207 us -> 12.7 us
  Pallas kernels: 0 us -> 101 us
  starting transfers between devices: 82.8 us -> 0.08 us
  local copies, waits for them, and re-layouts: 207 us -> 127 us
  waiting for transfers between devices: 295 us -> 325 us
    psum x11 -> x0, blocking collectives: 412 us -> none  [the longest x9 373 us: fine_sums(): return lax.psum(parts, ('wide', 'narrow'))]
    dot_general x362 -> x0, matrix products: 195 us -> none  [the longest x216 124 us: apply_taps(): jnp.dot(tap_window(padded, tap_id, extent), kernel[tap_id], preferred_ele...]
    pallas_call x0 -> x1, Pallas kernels: none -> 101 us  [step_call(): pl.pallas_call(functools.partial(step_kernel, cfg), out_shape=(jax.ShapeD...]
    ppermute x32 -> x0, starting transfers between devices: 82.8 us -> none  [the longest x16 62 us: extended(): lax.ppermute(tail, axis, [(i, (i + 1) % count) for i in range(ends)])]
    all_gather x1, waiting for transfers between devices: 61.7 us -> 96.3 us  [on_device(): lax.all_gather(params.astype(BF16), ('wide', 'narrow'), axis=0, tiled=True)]
    slice x69 -> x3, local copies, waits for them, and re-layouts: 35.1 us -> 5.81 us  [the longest x1 3.42 us: on_device(): gathered[SPLIT:]]
    another operation x54 -> x0, local copies, waits for them, and re-layouts: 21.7 us -> none
    concatenate x20 -> x2, other arithmetic: 7.71 us -> 24 us  [the longest x1 23.3 us: on_device(): weights = jnp.concatenate([part_a, part_b], 0)]
  transfers between devices with their start and end apart: 34 -> 2, of which waited for: 9 -> 2; matrix products, arithmetic and copies ran while one was open for 7% -> 1% of each run, Pallas kernels for 0% -> 0%
where the time goes in v1:
time: 794 us; the launch traced here: 779 us
  waiting for transfers between devices  325 us (41%)
  other arithmetic  158 us (20%)
  local copies, waits for them, and re-layouts  127 us (16%)
  Pallas kernels  101 us (13%)
  blocking collectives  40.1 us (5%)
  between operations  14.7 us (2%)
  matrix products  12.7 us (2%)
    unnamed x3, waiting for transfers between devices  229 us
    all_gather x1, other arithmetic, on_device(): lax.all_gather(params.astype(BF16), ('wide', 'narrow'), axis=0, tiled=True)  121 us
    concatenate x1, local copies, waits for them, and re-layouts, on_device(): jnp.concatenate([grads[ROW_IN:ROW_PSI].reshape(-1).astype(F32), small[16,...  103 us
    pallas_call x1, Pallas kernels, step_call(): pl.pallas_call(functools.partial(step_kernel, cfg), out_shape=(jax.ShapeD...  101 us
    all_gather x1, waiting for transfers between devices, on_device(): lax.all_gather(params.astype(BF16), ('wide', 'narrow'), axis=0, tiled=True)  96.3 us
    psum x1, blocking collectives, on_device(): weight_sq, update_sq = lax.psum((weight_sq, update_sq), ('wide', 'narrow'))  40.1 us
    concatenate x1, other arithmetic, on_device(): weights = jnp.concatenate([part_a, part_b], 0)  23.3 us
  transfers between devices with their start and end apart: 2, of which 2 were waited for; matrix products, arithmetic and copies ran while one was open for 1% of the time, Pallas kernels for 0%

profile of v1, /device:TPU:0, one launch (start us, length us, event | category | flops | bytes accessed | tf_op | source)
XLA Modules:
  0.0 778.6 jit_solution(3898405264278056832)
XLA Ops:
  7.2 1.0 convert_element_type.24
  8.2 0.9 reshape.56
  9.3 0.7 convert_element_type.23
  10.6 1.4 reshape.47.lab_ref
  12.1 0.7 bitcast_convert_fusion.2
  13.4 96.3 %all-gather.3.cloned.1.call-done = bf16[32,1,97792]{2,1,0:T(2,128)(2,1)} async-done(((bf16[1,1,97792]{2,1,0:T(2,128)(2,1)}), bf16[32,1,97792]{2,1,0:T(2,128)(2,1)}) %all-gather.3.cloned.1.call-update) | async-done | bytes 6258704 | tf_op jit(solution)/shard_map/all_gather | solution.py:810
  109.7 120.6 %reduce = bf16[32,97792]{1,0:T(8,128)(2,1)} reduce(bf16[32,1,97792]{2,1,0:T(2,128)(2,1)} %all-gather.3.cloned.1.call-done, bf16[]{:T(256)} %constant.57), dimensions={1}, to_apply=%all-gather.reduce_sub_computation | reduce | bytes 12517378 | tf_op jit(solution)/shard_map/all_gather | solution.py:810
  230.3 12.0 %reshape.57 = bf16[3129344]{0:T(1024)(128)(2,1)} reshape(bf16[32,97792]{1,0:T(8,128)(2,1)} %reduce) | data formatting | bytes 12517376
  242.3 3.4 slice.37
  245.7 1.9 slice.36
  247.6 1.4 pad_bitcast_fusion
  249.0 1.5 pad_bitcast_fusion.1
  250.5 23.3 %pad_maximum_fusion.w_ref = bf16[24480,128]{1,0:T(8,128)(2,1)} fusion(bf16[13872,128]{1,0:T(8,128)(2,1)S(1)} %pad_bitcast_fusion, bf16[10608,128]{1,0:T(8,128)(2,1)S(1)} %pad_bitcast_fusion.1), kind=kLoop, calls=%fused_computation | loop fusion | flops 12533760 | bytes 12533760 | tf_op jit(solution)/shard_map/concatenate | solution.py:818
  273.8 101.0 %shard_map.119 = (bf16[24480,128]{1,0:T(8,128)(2,1)}, f32[24,128]{1,0:T(8,128)}) custom-call(f32[16,128]{1,0:T(8,128)} %maximum_maximum_fusion.ct_ref, s32[1,512]{1,0:T(1,128)} %reshape.47.lab_ref, f32[1,512]{1,0:T(1,128)} %reshape.48.val_ref, bf16[24480,128]{1,0:T(8,128)(2,1)} %pad_maximum_fusion.w_ref), custom_call_target="tpu_custom_call" | custom-call | tf_op jit(solution)/shard_map/pallas_call | solution.py:788
  374.9 4.6 bitcast_convert_fusion
  379.4 3.9 bitcast_convert_fusion.1
  383.4 102.8 %concatenate.19 = f32[3129344]{0:T(1024)} concatenate(f32[1355136]{0:T(1024)} %bitcast_convert_fusion.1, f32[64]{0:T(128)S(1)} %multiply_bitcast_fusion.2, f32[1769472]{0:T(1024)} %bitcast_convert_fusion, f32[1923]{0:T(1024)S(1)} %slice_multiply_fusion, f32[2749]{0:T(1024)S(1)} %broadcast_in_dim.5), dimensions={0} | concatenate | bytes 25034752 | tf_op jit(solution)/shard_map/concatenate | solution.py:831
  486.3 228.8 %all-reduce.6.cloned.1.call-done = f32[3129344]{0:T(1024)} async-done(((f32[3129344]{0:T(1024)}), f32[3129344]{0:T(1024)}) %all-reduce.6.cloned.1.call-update) | async-done | bytes 12517392
  715.0 1.4 fusion.18
  717.0 4.3 fusion.13
  721.3 4.3 fusion.14
  726.2 40.1 %all-reduce.3 = (f32[12]{0:T(128)S(1)}, f32[12]{0:T(128)S(1)}) all-reduce(f32[12]{0:T(128)S(1)} %fusion.14, f32[12]{0:T(128)S(1)} %fusion.13), channel_id=1, replica_groups=mesh['wide'=8,'narrow'=4] {'wide','narrow'}, use_global_device_ids=true, to_apply=%region_2.0 | all-reduce | flops 24 | bytes 192 | tf_op jit(solution)/shard_map/psum | solution.py:859
  766.3 4.1 fusion.12
  770.4 1.0 multiply_subtract_fusion
  (32 shorter events, 2.7 us)
Async XLA Ops:
  7.2 102.5 %all-gather.3.cloned.1.call-start = ((), (), s32[]{:S(2)}) async-start(), calls=%async_computation | async-start | bytes 12908544 | tf_op jit(solution)/shard_map/all_gather | solution.py:810
  9.2 705.8 %all-reduce.6.cloned.1.call-start = ((), (), s32[]{:S(2)}) async-start(), calls=%async_computation.1 | async-start | bytes 25034752
  379.4 3.9 copy-start.5
  486.2 228.9 %copy-start = (f32[97792]{0:T(1024)S(1)}, f32[97792]{0:T(1024)}, u32[]{:S(2)}) copy-start(f32[97792]{0:T(1024)} %param.8) | copy-start | bytes 1173508
  486.2 228.9 %copy-start.3 = (f32[97792]{0:T(1024)S(1)}, f32[97792]{0:T(1024)}, u32[]{:S(2)}) copy-start(f32[97792]{0:T(1024)} %param.9) | copy-start | bytes 1173508
  486.2 228.9 %copy-start.4 = (f32[97792]{0:T(1024)S(1)}, f32[97792]{0:T(1024)}, u32[]{:S(2)}) copy-start(f32[97792]{0:T(1024)} %param.10) | copy-start | bytes 1173508
  486.2 230.8 %copy-start.6 = (s32[12]{0:T(128)S(1)}, s32[12]{0:T(128)}, u32[]{:S(2)}) copy-start(s32[12]{0:T(128)} %constant.45.clone) | copy-start | bytes 148
  486.2 230.8 %copy-start.7 = (s32[12]{0:T(128)S(1)}, s32[12]{0:T(128)}, u32[]{:S(2)}) copy-start(s32[12]{0:T(128)} %constant.46.clone) | copy-start | bytes 148
  716.4 53.9 %copy-start.1 = (f32[97792]{0:T(1024)}, f32[97792]{0:T(1024)S(1)}, u32[]{:S(2)}) copy-start(f32[97792]{0:T(1024)S(1)} %get-tuple-element.12) | copy-start | bytes 1173508
  716.4 53.9 %copy-start.2 = (f32[97792]{0:T(1024)}, f32[97792]{0:T(1024)S(1)}, u32[]{:S(2)}) copy-start(f32[97792]{0:T(1024)S(1)} %get-tuple-element.13) | copy-start | bytes 1173508
Sparse Core Ops, SparseCore 0:
  11.4 98.2 all-gather.2
  486.3 228.6 all-reduce.5

commit v2 on v1

--- a/solution.py
+++ b/solution.py
@@ -58,8 +58,43 @@
 
 DIRS = tuple((dx, dy) for dx in (-1, 0, 1) for dy in (-1, 0, 1) if (dx, dy) != (0, 0))
 
-N_AR = 10
+N_AR = 11
 N_HALO = 9
+PIECES = 3
+
+
+def grid_of(nw, nn):
+    nx = max(k for k in range(1, nw + 1) if nw % k == 0 and k * k <= nw)
+    ny = max(nn // 2, 1)
+    return nw // nx, nx, ny, nn // ny
+
+
+class Layout:
+    def __init__(self, shard_len, total):
+        self.rows = shard_len // LANES
+        self.total = total
+        self.turn = -(-SPLIT // shard_len)
+        self.shift_a = FRONT // LANES
+        self.shift_b = ROWS_A - SPLIT // LANES - 1
+        begin = [self.first(p) for p in range(total + 1)]
+        edge = []
+        for p in range(1, total + 1):
+            low = self.rows * p + (self.shift_b if p >= self.turn else self.shift_a)
+            edge.append(low // 16)
+        self.body = min(edge[p] - begin[p] for p in range(total))
+        self.gap = max(begin[p + 1] - begin[p] - self.body for p in range(total))
+        self.begin = begin
+        self.half = -(-self.body // 2)
+        self.fix = 16 * (1 + self.gap)
+        self.window = 16 * (1 + self.body + self.gap)
+        self.window += 16 * ((self.window // 16) % 2)
+        self.weight_rows = 16 * begin[total]
+        self.grad_rows = max(16 * (begin[p] - 1) for p in range(total)) + self.window
+        self.grad_rows = max(self.grad_rows, self.weight_rows)
+
+    def first(self, p):
+        late = (p + self.total - self.turn) // self.total
+        return (self.rows * p + self.shift_a + 15 + (self.shift_b + 1 - self.shift_a) * late) // 16
 
 
 def dot(a, b):
@@ -86,9 +121,24 @@
     return s * (1.0 + v * (1.0 - s))
 
 
-def step_kernel(cfg, ct_ref, lab_ref, val_ref, w_ref, g_ref, out_ref, *scr):
+def step_kernel(
+    cfg,
+    ct_ref,
+    lab_ref,
+    val_ref,
+    param_ref,
+    first_ref,
+    second_ref,
+    param_out,
+    first_out,
+    second_out,
+    scalar_out,
+    *scr,
+):
     names = cfg["names"]
     s = dict(zip(names, scr))
+    w_ref, g_ref = s["weights"], s["grads"]
+    lay = cfg["lay"]
     nw, nn = cfg["nw"], cfg["nn"]
     total = nw * nn
     X, Y, Z = cfg["ext"]
@@ -114,7 +164,292 @@
         return carry
 
     lax.fori_loop(1, total, greet, 0)
+
+    nz, nx, ny, nc = grid_of(nw, nn)
+    here = (w // nx, lax.rem(w, nx), n // nc, lax.rem(n, nc))
+    sizes = (nz, nx, ny, nc)
+
+    def place(r):
+        z, x, y, c = [
+            h if d == 0 else lax.rem(h + d % k, k) for h, d, k in zip(here, r, sizes)
+        ]
+        return z * nx + x, y * nc + c
+
+    def number(r):
+        a, b = place(r)
+        return a * nn + b
+
+    natural = s["natural"]
+    lead = 32
+    natural[0:lead] = jnp.zeros((lead, LANES), F32)
+    natural[lead : lead + lay.rows] = param_ref[...]
+    rest = natural.shape[0] - lead - lay.rows
+    natural[lead + lay.rows :] = jnp.zeros((rest, LANES), F32)
+    begin = lay.first(me)
+    off_a = lay.rows * me + lay.shift_a - 16 * (begin - 1)
+    off_b = off_a + lay.shift_b - lay.shift_a
+    lane = iota((1, LANES), 1)
+    span = 16 * (1 + lay.body + lay.gap)
+    row_at = iota((span, LANES), 0) + 16 * (begin - 1)
+    as_a = natural[pl.ds(lead - off_a, span), :]
+    late = pltpu.roll(natural[pl.ds(lead - off_b, span), :], LANES // 2, 1)
+    early = pltpu.roll(natural[pl.ds(lead - off_b - 1, span), :], LANES // 2, 1)
+    as_b = jnp.where(lane < LANES // 2, early, late)
+    share = jnp.where(row_at < ROWS_A, as_a, as_b).astype(BF16)
+    fix = s["fix"]
+    body = 16 * lay.body
+
+    def at_tile(t):
+        return pl.multiple_of(16 * t, 16)
+
+    w_ref[pl.ds(at_tile(begin), body), :] = share[16 : 16 + body]
+    fix[me] = jnp.concatenate([share[0:16], share[16 + body : 16 + body + 16 * lay.gap]], 0)
     pl.semaphore_wait(barrier, total - 1)
+
+    gather_send, gather_recv = s["gather_send"], s["gather_recv"]
+    sent = [0] * PIECES
+
+    def flat_id(r):
+        z, x, y, c = [d % k for d, k in zip(r, sizes)]
+        return ((z * nx + x) * ny + y) * nc + c
+
+    def piece_ref(r, piece):
+        p = number(r)
+        if piece == 2:
+            return fix.at[p]
+        lo = 0 if piece == 0 else lay.half
+        size = lay.half if piece == 0 else lay.body - lay.half
+        return w_ref.at[pl.ds(at_tile(lay.first(p) + lo), 16 * size)]
+
+    def gather_copy(r, d, piece):
+        ref = piece_ref(r, piece)
+        there = tuple(a - b for a, b in zip(r, d))
+        return pltpu.make_async_remote_copy(
+            ref,
+            ref,
+            gather_send.at[piece],
+            gather_recv.at[flat_id(there), piece],
+            device_id=place(d),
+            device_id_type=MESH,
+        )
+
+    def gather_push(r, dests, pieces):
+        for d in dests:
+            for piece in pieces:
+                gather_copy(r, d, piece).start()
+                sent[piece] += 1
+
+    def gather_take(r):
+        for piece in range(PIECES):
+            gather_copy(r, (0, 0, 0, 0), piece).wait_recv()
+
+    along_z = [(k, 0, 0, 0) for k in range(1, nz)]
+    along_x = [(0, k, 0, 0) for k in range(1, nx)]
+    along_y = [(0, 0, k, 0) for k in range(1, ny)]
+    sibling = [(0, 0, 0, k) for k in range(1, nc)]
+    every = (0, 1, 2)
+    gather_push((0, 0, 0, 0), along_x + along_y + along_z + sibling, every)
+    for kz in range(nz):
+        if kz:
+            gather_take((kz, 0, 0, 0))
+            gather_push((kz, 0, 0, 0), along_x + along_y + sibling, every)
+        for kx in range(1, nx):
+            gather_take((kz, kx, 0, 0))
+            gather_push((kz, kx, 0, 0), along_y, (0, 2))
+            gather_push((kz, kx, 0, 0), sibling, every)
+        for ky in range(1, ny):
+            gather_take((kz, 0, ky, 0))
+            gather_push((kz, 0, ky, 0), along_x, (1,))
+            gather_push((kz, 0, ky, 0), sibling, every)
+    for kz in range(nz):
+        for kx in range(1, nx):
+            for ky in range(1, ny):
+                gather_take((kz, kx, ky, 0))
+                gather_push((kz, kx, ky, 0), sibling, every)
+    for kz in range(nz):
+        for kx in range(nx):
+            for ky in range(ny):
+                for kc in range(1, nc):
+                    gather_take((kz, kx, ky, kc))
+    for p in range(total):
+        tile = lay.begin[p] + lay.body
+        if p == 0:
+            w_ref[16 * (lay.begin[0] - 1) : 16 * lay.begin[0]] = fix[0, 0:16]
+        for i in range(lay.begin[p + 1] - tile):
+            part = fix[p, 16 * (1 + i) : 16 * (2 + i)]
+            if tile + i == lay.begin[p + 1] - 1 and p + 1 < total:
+                part = part + fix[p + 1, 0:16]
+            w_ref[16 * (tile + i) : 16 * (tile + i + 1)] = part
+
+    def gather_end():
+        for piece, count in enumerate(sent):
+            if piece == 2:
+                ref = fix
+                unit = 1
+            else:
+                ref = w_ref
+                unit = 16 * (lay.half if piece == 0 else lay.body - lay.half)
+            most = ref.shape[0] // unit
+            while count:
+                k = min(count, most)
+                whole = ref.at[pl.ds(0, k * unit)]
+                pltpu.make_async_remote_copy(
+                    whole,
+                    whole,
+                    gather_send.at[piece],
+                    gather_recv.at[0, piece],
+                    device_id=(w, n),
+                    device_id_type=MESH,
+                ).wait_send()
+                count -= k
+
+    cc, dx_in, dy_in = s["red_c"], s["red_dx"], s["red_dy"]
+    ex_in, ey_in, zz_in = s["red_ex"], s["red_ey"], s["red_z"]
+    red_send, red_recv = s["red_send"], s["red_recv"]
+    win_rows = lay.window
+    mid_row = win_rows // 2
+    halves = (pl.ds(0, mid_row), pl.ds(mid_row, mid_row))
+    started = []
+
+    def grad_window(r_abs_z, rx, ry, rc):
+        x = lax.rem(here[1] + rx, nx) if rx else here[1]
+        y = lax.rem(here[2] + ry, ny) if ry else here[2]
+        c = lax.rem(here[3] + rc, nc) if rc else here[3]
+        p = (r_abs_z * nx + x) * nn + y * nc + c
+        return pl.ds(at_tile(lay.first(p) - 1), win_rows)
+
+    tags = {}
+
+    def tag(key):
+        return tags.setdefault(key, len(tags))
+
+    def red_copy(src, dst, key, d):
+        i = tag(key)
+        return pltpu.make_async_remote_copy(
+            src, dst, red_send.at[i], red_recv.at[i], device_id=place(d), device_id_type=MESH
+        )
+
+    def red_go(*a):
+        copy = red_copy(*a)
+        copy.start()
+        started.append(copy)
+
+    def red_one(zd, rx, ry):
+        return [
+            (g_ref.at[grad_window(zd, rx, ry, k)], cc.at[zd, rx, ry, k - 1], (1, zd, rx, ry, k), (0, 0, 0, k))
+            for k in range(1, nc)
+        ]
+
+    def others(size):
+        return range(1, size)
+
+    def red_two(zd):
+        moves = []
+        for rx in others(nx):
+            for ry in others(ny):
+                moves.append(
+                    (cc.at[zd, rx, ry, 0, halves[0]], dx_in.at[zd, nx - rx - 1, ry - 1],
+                     (2, zd, nx - rx, ry, 0), (0, rx, 0, 0))
+                )
+                moves.append(
+                    (cc.at[zd, rx, ry, 0, halves[1]], dy_in.at[zd, rx - 1, ny - ry - 1],
+                     (2, zd, rx, ny - ry, 1), (0, 0, ry, 0))
+                )
+        return moves
+
+    def red_three(zd):
+        moves = []
+        for rx in others(nx):
+            moves.append((cc.at[zd, rx, 0, 0], ex_in.at[zd, nx - rx - 1], (3, zd, nx - rx, 0), (0, rx, 0, 0)))
+        for ry in others(ny):
+            moves.append((cc.at[zd, 0, ry, 0], ey_in.at[zd, ny - ry - 1], (3, zd, 0, ny - ry), (0, 0, ry, 0)))
+        return moves
+
+    def red_start_one(planes):
+        for zd in planes:
+            for rx in range(nx):
+                for ry in range(ny):
+                    for move in red_one(zd, rx, ry):
+                        red_go(*move)
+
+    def red_end_one(planes):
+        for zd in planes:
+            for rx in range(nx):
+                for ry in range(ny):
+                    for move in red_one(zd, rx, ry):
+                        red_copy(*move).wait_recv()
+                    total_w = g_ref[grad_window(zd, rx, ry, 0), :].astype(F32)
+                    for k in range(1, nc):
+                        total_w = total_w + cc[zd, rx, ry, k - 1].astype(F32)
+                    cc[zd, rx, ry, 0] = total_w.astype(BF16)
+            for move in red_two(zd):
+                red_go(*move)
+
+    def red_end_two(planes):
+        for zd in planes:
+            for move in red_two(zd):
+                red_copy(*move).wait_recv()
+            for ry in others(ny):
+                part = cc[zd, 0, ry, 0, halves[0]].astype(F32)
+                for sx in others(nx):
+                    part = part + dx_in[zd, sx - 1, ry - 1].astype(F32)
+                cc[zd, 0, ry, 0, halves[0]] = part.astype(BF16)
+            for rx in others(nx):
+                part = cc[zd, rx, 0, 0, halves[1]].astype(F32)
+                for sy in others(ny):
+                    part = part + dy_in[zd, rx - 1, sy - 1].astype(F32)
+                cc[zd, rx, 0, 0, halves[1]] = part.astype(BF16)
+            for move in red_three(zd):
+                red_go(*move)
+
+    def red_last(zd, k):
+        return pltpu.make_async_remote_copy(
+            cc.at[zd, 0, 0, 0],
+            zz_in.at[nz - k - 1],
+            red_send.at[tag((4, zd))],
+            red_recv.at[tag((5, nz - k))],
+            device_id=place((k, 0, 0, 0)),
+            device_id_type=MESH,
+        )
+
+    def red_end_three(planes):
+        for zd in planes:
+            for move in red_three(zd):
+                red_copy(*move).wait_recv()
+            part = cc[zd, 0, 0, 0].astype(F32)
+            for sx in others(nx):
+                part = part + ex_in[zd, sx - 1].astype(F32)
+            for sy in others(ny):
+                part = part + ey_in[zd, sy - 1].astype(F32)
+            cc[zd, 0, 0, 0] = part.astype(BF16)
+            for k in others(nz):
+
+                @pl.when(lax.rem(here[0] + k, nz) == zd)
+                def _():
+                    red_last(zd, k).start()
+
+    acc = s["acc"]
+
+    def red_end_last(planes):
+        for zd in planes:
+
+            @pl.when(here[0] == zd)
+            def _():
+                part = cc[zd, 0, 0, 0].astype(F32)
+                for k in others(nz):
+                    red_last(zd, nz - k).wait_recv()
+                for k in others(nz):
+                    part = part + zz_in[k - 1].astype(F32)
+                acc[16 : 16 + win_rows] = part
+
+    def red_finish():
+        for copy in started:
+            copy.wait_send()
+        for zd in range(nz):
+
+            @pl.when(here[0] != zd)
+            def _():
+                red_last(zd, 1).wait_send()
 
     slots, ar_send, ar_recv = s["slots"], s["ar_send"], s["ar_recv"]
 
@@ -307,6 +642,15 @@
         mean = jnp.concatenate(parts[:half], 1) / count
         spread_v = jnp.concatenate(parts[half:], 1) / count - mean * mean
         return mean, lax.rsqrt(spread_v + EPS_NORM)
+
+    def last_of(zd):
+        low = 16 * (lay.begin[zd * nx * nn] - 1)
+        return 2 if low < ROW_MID else 1 if low < ROW_PSI else 0
+
+    wave_a, wave_b, wave_c = [[zd for zd in range(nz) if last_of(zd) == k] for k in range(3)]
+    g_ref[0:32] = jnp.zeros((32, LANES), BF16)
+    g_ref[ROW_PSI:ROWS_A] = jnp.zeros((ROWS_A - ROW_PSI, LANES), BF16)
+    g_ref[ROW_TAIL:] = jnp.zeros((g_ref.shape[0] - ROW_TAIL, LANES), BF16)
 
     cts, ct_send, ct_recv = s["cts"], s["ct_send"], s["ct_recv"]
     cts[4] = ct_ref[...]
@@ -633,6 +977,7 @@
         dot_tn(skip_own.astype(BF16), low_fine), C1 // 2
     )
     g_ref[ROW_G : ROW_G + C2 // 2, :] = narrow_back(dot_tn(coarse_own, low_gc), C2 // 2)
+    red_start_one(wave_a)
     sums, back = norm_back_end(7, 7, raw3, mean3, inv3, gain[2], coarse_voxels, ("dy3", "dyl3"))
     grad_shift[2], grad_gain[2] = [sums[0:1], sums[1:2]], [sums[2:3], sums[3:4]]
     dpad = s["dpad3"]
@@ -654,18 +999,25 @@
             stacked = jnp.concatenate([stacked[:, 0:C1], stacked[:, C1:C2]], 0)
             lo = ROW_MID + (3 * ab + c) * C2
             g_ref[lo : lo + C2, :] = dot(shuffle, stacked).astype(BF16)
+    red_end_one(wave_a)
+    red_start_one(wave_b)
     sums, back = norm_back_end(8, 8, raw2, mean2, inv2, gain[1], voxels, ("dy2", "dyl2"))
     grad_shift[1], grad_gain[1] = [sums[0:1]], [sums[1:2]]
     dpad = s["dpad2"]
     put_three(dpad, back, 0, C1)
     clear_edges(dpad, 1)
     low_raw2 = flat(own(dpad)[:, :, :, C1 : 2 * C1])
+    red_end_two(wave_a)
+    red_end_one(wave_b)
     grad_act = conv_back(dpad, w_ref, ROW_ENC, C1, C1, (X, Y))
     hat1 = (flat(own(raw1)) - mean1) * inv1
     v = hat1 * gain[0] + shift[0]
     dy = grad_act * silu_grad(v, jax.nn.sigmoid(v))
     ar_start(9, [col_sum(dy), col_sum(dy * hat1)])
     conv_grad(pad1, low_raw2, ROW_ENC, (X, Y))
+    red_start_one(wave_c)
+    red_end_three(wave_a)
+    red_end_two(wave_b)
     sums = ar_wait(9)
     grad_shift[0], grad_gain[0] = [sums[0:1]], [sums[1:2]]
     back = inv1 * gain[0] * (dy - sums[0:1] / voxels - hat1 * (sums[1:2] / voxels))
@@ -678,7 +1030,33 @@
         for c in range(3):
             in_rows.append(col_sum(block[c * Z : (c + 1) * Z]))
     in_rows = [jnp.zeros((ROW_IN, LANES), F32)] + in_rows
-    g_ref[0:32, :] = jnp.concatenate(in_rows, 0).astype(BF16)
+    in_slots, in_send, in_recv = s["in_slots"], s["in_send"], s["in_recv"]
+    in_slots[me] = jnp.concatenate(in_rows, 0).astype(BF16)
+
+    def in_copy():
+        return pltpu.make_async_remote_copy(
+            in_slots.at[me],
+            in_slots.at[me],
+            in_send,
+            in_recv,
+            device_id=(0, 0),
+            device_id_type=MESH,
+        )
+
+    def in_whole():
+        others_in = in_slots.at[pl.ds(0, total - 1)]
+        return pltpu.make_async_remote_copy(
+            others_in, others_in, in_send, in_recv, device_id=(w, n), device_id_type=MESH
+        )
+
+    @pl.when(me != 0)
+    def _():
+        in_copy().start()
+
+    red_end_one(wave_c)
+    red_end_last(wave_a)
+    red_end_three(wave_b)
+    red_end_two(wave_c)
 
     side_whole().wait_recv()
     small = jnp.sum(side[...], axis=0)
@@ -704,16 +1082,86 @@
     for q in range(1, 12):
         flat_rows.append(jnp.where(lane_id < used_lanes, later[q - 1], later[q]))
     flat_rows.append(jnp.where(lane_id < used_lanes, later[11], 0.0))
-    out_ref[0:16] = jnp.concatenate(flat_rows, 0)
-    out_ref[16:24] = jnp.concatenate(
-        [
-            jnp.where(lane_id < GATE, small[4:5], 0.0),
-            loss_row,
-            jnp.broadcast_to(valid_count, (1, LANES)),
-            jnp.zeros((5, LANES), F32),
-        ],
-        0,
+    tail_grad = jnp.concatenate(flat_rows, 0)
+    psi_row = jnp.where(lane_id < GATE, small[4:5], 0.0)
+    scalar_out[...] = jnp.concatenate(
+        [loss_row, jnp.broadcast_to(valid_count, (1, LANES)), jnp.zeros((6, LANES), F32)], 0
     )
+
+    red_end_three(wave_c)
+    red_end_last(wave_b)
+    red_end_last(wave_c)
+
+    base = 16 * (begin - 1) - 16
+
+    def put_row(row, block):
+        at = row - base
+        rows = block.shape[0]
+
+        @pl.when((at >= 16) & (at + rows <= 16 + win_rows))
+        def _():
+            acc[pl.ds(pl.multiple_of(at, 16), rows), :] = block
+
+    put_row(ROW_TAIL, tail_grad)
+    put_row(ROW_PSI, jnp.concatenate([psi_row, jnp.zeros((15, LANES), F32)], 0))
+
+    @pl.when(me == 0)
+    def _():
+        in_whole().wait_recv()
+        at = 16 - 16 * (lay.begin[0] - 1)
+        acc[at : at + 32] = acc[at : at + 32] + jnp.sum(in_slots[...].astype(F32), axis=0)
+
+    grad_a = acc[pl.ds(16 + off_a, lay.rows), :]
+    late = pltpu.roll(acc[pl.ds(16 + off_b + 1, lay.rows), :], LANES // 2, 1)
+    early = pltpu.roll(acc[pl.ds(16 + off_b, lay.rows), :], LANES // 2, 1)
+    grad_b = jnp.where(lane < LANES // 2, early, late)
+    position = (
+        me * lay.rows * LANES
+        + iota((lay.rows, LANES), 0) * LANES
+        + iota((lay.rows, LANES), 1)
+    )
+    gradient = jnp.where(position < SPLIT, grad_a, grad_b)
+    gradient = jnp.where(position < USED, gradient, 0.0)
+    params = param_ref[...]
+    new_first = BETA_ONE * first_ref[...] + (1.0 - BETA_ONE) * gradient
+    new_second = BETA_TWO * second_ref[...] + (1.0 - BETA_TWO) * gradient * gradient
+    first_out[...] = new_first
+    second_out[...] = new_second
+    update = (
+        new_first
+        / (1.0 - BETA_ONE**STEP)
+        / (jnp.sqrt(new_second / (1.0 - BETA_TWO**STEP)) + EPS_ADAM)
+        + DECAY_RATE * params
+    )
+    param_out[...] = update
+    limits = STARTS + (USED, total * lay.rows * LANES)
+    squares = (params * params, update * update)
+    lines = []
+    for square in squares:
+        for k in range(len(limits) - 1):
+            member = (position >= limits[k]) & (position < limits[k + 1])
+            lines.append(col_sum(jnp.where(member, square, 0.0)))
+    lines = jnp.concatenate(lines, 0)
+    lines = jnp.sum(lines, axis=1, keepdims=True)
+    k = lines.shape[0]
+    line = col_sum(jnp.where(iota((k, LANES), 0) == iota((k, LANES), 1), lines, 0.0))
+    ar_start(10, [line])
+    sums = ar_wait(10)[0:1]
+    parts = len(limits) - 1
+    roots = jnp.sqrt(sums)
+    scale = jnp.zeros((lay.rows, LANES), F32)
+    for k in range(parts):
+        member = (position >= limits[k]) & (position < limits[k + 1])
+        ratio = roots[:, k : k + 1] / roots[:, parts + k : parts + k + 1]
+        scale = jnp.where(member, ratio, scale)
+    param_out[...] = param_ref[...] - LEARN_RATE * scale * param_out[...]
+
+    gather_end()
+    red_finish()
+
+    @pl.when(me != 0)
+    def _():
+        in_copy().wait_send()
 
     for r in range(N_AR):
         ar_whole(r).wait_send()
@@ -727,7 +1175,7 @@
             halo_copy(h, s[name], i).wait_send()
 
 
-def step_call(nw, nn, ext, ct, lab, val, weights):
+def step_call(nw, nn, ext, ct, lab, val, params, first, second):
     X, Y, Z = ext
     XE, YE = X + 2, Y + 2
     CX, CY, CZ = X // 2, Y // 2, Z // 2
@@ -735,7 +1183,31 @@
     framed = (XE, YE, Z)
     small = (CX + 2, CY + 2, CZ)
     dma = pltpu.SemaphoreType.DMA
+    rows = params.shape[0]
+    lay = Layout(rows * LANES, total)
+    nz, nx, ny, nc = grid_of(nw, nn)
+    ox, oy = max(nx - 1, 1), max(ny - 1, 1)
+    n_red = nz * (nx * ny * (nc - 1) + 2 * (nx - 1) * (ny - 1) + nx + ny) + 2 * nz + 8
+    low = lambda *shape: pltpu.VMEM(shape, BF16)
     scratch = {
+        "weights": low(lay.weight_rows, LANES),
+        "grads": low(lay.grad_rows, LANES),
+        "natural": pltpu.VMEM((rows + 112, LANES), F32),
+        "fix": low(total, lay.fix, LANES),
+        "gather_send": dma((PIECES,)),
+        "gather_recv": dma((total, PIECES)),
+        "red_c": low(nz, nx, ny, nc - 1, lay.window, LANES),
+        "red_dx": low(nz, ox, oy, lay.window // 2, LANES),
+        "red_dy": low(nz, ox, oy, lay.window // 2, LANES),
+        "red_ex": low(nz, ox, lay.window, LANES),
+        "red_ey": low(nz, oy, lay.window, LANES),
+        "red_z": low(nz, lay.window, LANES),
+        "red_send": dma((n_red,)),
+        "red_recv": dma((n_red,)),
+        "acc": pltpu.VMEM((lay.window + 48, LANES), F32),
+        "in_slots": low(total, 32, LANES),
+        "in_send": dma,
+        "in_recv": dma,
         "slots": pltpu.VMEM((N_AR, total, 4, LANES), F32),
         "ar_send": dma((N_AR,)),
         "ar_recv": dma((N_AR,)),
@@ -783,86 +1255,47 @@
         "dpad2": pltpu.VMEM(framed + (3 * C1,), BF16),
         "d_skip": pltpu.VMEM((X * Y * Z, C1), F32),
     }
-    cfg = {"nw": nw, "nn": nn, "ext": ext, "names": tuple(scratch)}
+    cfg = {"nw": nw, "nn": nn, "ext": ext, "names": tuple(scratch), "lay": lay}
     vmem = pl.BlockSpec(memory_space=pltpu.VMEM)
     return pl.pallas_call(
         functools.partial(step_kernel, cfg),
         out_shape=(
-            jax.ShapeDtypeStruct(weights.shape, BF16),
-            jax.ShapeDtypeStruct((24, LANES), F32),
+            jax.ShapeDtypeStruct((rows, LANES), F32),
+            jax.ShapeDtypeStruct((rows, LANES), F32),
+            jax.ShapeDtypeStruct((rows, LANES), F32),
+            jax.ShapeDtypeStruct((8, LANES), F32),
         ),
-        in_specs=[vmem] * 4,
-        out_specs=(vmem, vmem),
+        in_specs=[vmem] * 6,
+        out_specs=(vmem,) * 4,
         scratch_shapes=list(scratch.values()),
         compiler_params=pltpu.CompilerParams(
             collective_id=0, has_side_effects=True, vmem_limit_bytes=60 * 1024 * 1024
         ),
-    )(ct, lab, val, weights)
+    )(ct, lab, val, params, first, second)
 
 
 def on_device(params, first_moment, second_moment, ct_image, labels, valid_mask):
-    shard_len = params.shape[0]
-    n_wide = lax.axis_size("wide")
-    n_narrow = lax.axis_size("narrow")
-    devices = n_wide * n_narrow
-    place = lax.axis_index(("wide", "narrow"))
     ext = ct_image.shape
-    gathered = lax.all_gather(params.astype(BF16), ("wide", "narrow"), axis=0, tiled=True)
-    part_a = jnp.concatenate(
-        [jnp.zeros((FRONT,), BF16), gathered[: ROWS_A * LANES - FRONT]]
-    ).reshape(-1, LANES)
-    n_b = -(-(shard_len * devices - SPLIT) // TILE) * TILE
-    part_b = jnp.concatenate(
-        [gathered[SPLIT:], jnp.zeros((n_b - (shard_len * devices - SPLIT),), BF16)]
-    ).reshape(-1, LANES)
-    weights = jnp.concatenate([part_a, part_b], 0)
     ct = ct_image.astype(F32).reshape(-1, ext[2])
     ct = jnp.concatenate([ct, ct, ct, jnp.zeros((ct.shape[0], LANES - 3 * ext[2]), F32)], 1)
-    grads, small = step_call(
-        n_wide,
-        n_narrow,
+    new_params, new_first, new_second, scalars = step_call(
+        lax.axis_size("wide"),
+        lax.axis_size("narrow"),
         ext,
         ct,
         labels.reshape(1, -1),
         valid_mask.astype(F32).reshape(1, -1),
-        weights,
+        params.reshape(-1, LANES),
+        first_moment.reshape(-1, LANES),
+        second_moment.reshape(-1, LANES),
     )
-    first = (place == 0).astype(F32)
-    flat_grad = jnp.concatenate(
-        [
-            grads[ROW_IN:ROW_PSI].reshape(-1).astype(F32),
-            small[16, :GATE] * first,
-            grads[ROW_DEC1:ROW_TAIL].reshape(-1).astype(F32),
-            small[0:16].reshape(-1)[: USED - STARTS[8]] * first,
-            jnp.zeros((shard_len * devices - USED,), F32),
-        ]
+    return (
+        new_params.reshape(-1),
+        new_first.reshape(-1),
+        new_second.reshape(-1),
+        scalars[0, 0],
+        scalars[1, 0],
     )
-    loss_sum = small[17, 0]
-    valid_count = small[18, 0]
-    gradient = lax.psum_scatter(flat_grad, ("wide", "narrow"), scatter_dimension=0, tiled=True)
-    new_first = BETA_ONE * first_moment + (1.0 - BETA_ONE) * gradient
-    new_second = BETA_TWO * second_moment + (1.0 - BETA_TWO) * gradient * gradient
-    update = (
-        new_first
-        / (1.0 - BETA_ONE**STEP)
-        / (jnp.sqrt(new_second / (1.0 - BETA_TWO**STEP)) + EPS_ADAM)
-        + DECAY_RATE * params
-    )
-    seg_lower = jnp.array(STARTS + (USED,), jnp.int32)
-    seg_upper = jnp.array(STARTS[1:] + (USED, shard_len * devices), jnp.int32)
-    position = place * shard_len + lax.iota(jnp.int32, shard_len)
-    member_map = (
-        (position[:, None] >= seg_lower[None]) & (position[:, None] < seg_upper[None])
-    ).astype(F32)
-    weight_sq = jnp.dot(params * params, member_map, precision=lax.Precision.HIGHEST)
-    update_sq = jnp.dot(update * update, member_map, precision=lax.Precision.HIGHEST)
-    weight_sq, update_sq = lax.psum((weight_sq, update_sq), ("wide", "narrow"))
-    trust_ratio = jnp.sqrt(weight_sq) / jnp.sqrt(update_sq)
-    new_params = (
-        params
-        - LEARN_RATE * jnp.dot(member_map, trust_ratio, precision=lax.Precision.HIGHEST) * update
-    )
-    return (new_params, new_first, new_second, loss_sum, valid_count)
 
 
 def solution(mesh):

time: 794 us -> 198 us (0.25); the launches traced: 779 us -> 198 us
  waiting for transfers between devices: 325 us -> 0 us
  other arithmetic: 158 us -> 1.37 us
  local copies, waits for them, and re-layouts: 127 us -> 6.45 us
  Pallas kernels: 101 us -> 189 us
  blocking collectives: 40.1 us -> 0 us
  between operations: 14.7 us -> 0.65 us
  matrix products: 12.7 us -> 0 us
    unnamed x3 -> x0, waiting for transfers between devices: 229 us -> none
    all_gather x1 -> x0, other arithmetic: 121 us -> none  [on_device(): lax.all_gather(params.astype(BF16), ('wide', 'narrow'), axis=0, tiled=True)]
    concatenate x1 -> x0, local copies, waits for them, and re-layouts: 103 us -> none  [on_device(): jnp.concatenate([grads[ROW_IN:ROW_PSI].reshape(-1).astype(F32), small[16,...]
    all_gather x1 -> x0, waiting for transfers between devices: 96.3 us -> none  [on_device(): lax.all_gather(params.astype(BF16), ('wide', 'narrow'), axis=0, tiled=True)]
    pallas_call x1, Pallas kernels: 101 us -> 189 us  [step_call(): pl.pallas_call(functools.partial(step_kernel, cfg), out_shape=(jax.ShapeD...]
    psum x1 -> x0, blocking collectives: 40.1 us -> none  [on_device(): weight_sq, update_sq = lax.psum((weight_sq, update_sq), ('wide', 'narrow'))]
    concatenate x1 -> x0, other arithmetic: 23.3 us -> none  [on_device(): weights = jnp.concatenate([part_a, part_b], 0)]
    dot_general x3 -> x0, matrix products: 12.7 us -> none  [the longest x1 4.32 us: on_device(): jnp.dot(update * update, member_map, precision=lax.Precision.HIGHEST)]
  transfers between devices with their start and end apart: 2 -> 0, of which waited for: 2 -> 0; matrix products, arithmetic and copies ran while one was open for 1% -> 0% of each run, Pallas kernels for 0% -> 0%
where the time goes in v2:
time: 198 us
  Pallas kernels  189 us (95%)
  local copies, waits for them, and re-layouts  6.45 us (3%)
    pallas_call x1, Pallas kernels, step_call(): pl.pallas_call(functools.partial(step_kernel, cfg), out_shape=(jax.ShapeD...  189 us

profile of v2, /device:TPU:0, one launch (start us, length us, event | category | flops | bytes accessed | tf_op | source)
XLA Modules:
  0.0 197.9 jit_solution(18121063002110061519)
XLA Ops:
  0.6 0.7 bitcast_convert_fusion
  1.3 0.1 pad.3.clone
  1.4 0.0 copy-start.3
  1.4 0.7 maximum_maximum_fusion.ct_ref
  2.1 0.0 copy-done.3
  2.1 0.0 copy-start.2
  2.1 0.7 reshape.43.val_ref
  2.8 0.0 copy-done.2
  2.8 0.7 reshape.42.lab_ref
  3.5 189.4 %shard_map.101 = (f32[764,128]{1,0:T(8,128)}, f32[764,128]{1,0:T(8,128)}, f32[764,128]{1,0:T(8,128)}, f32[8,128]{1,0:T(8,128)}) custom-call(f32[16,128]{1,0:T(8,128)} %maximum_maximum_fusion.ct_ref, s32[1,512]{1,0:T(1,128)} %reshape.42.lab_ref, f32[1,512]{1,0:T(1,128)} %reshape.43.val_ref, f32[764,128]{1,0:T(8,128)} %bitcast.14, f32[764,128]{1,0:T(8,128)} %bitcast.15, ...), custom_call_target="tpu_custom_call" | custom-call | tf_op jit(solution)/shard_map/pallas_call | solution.py:1260
  192.9 1.3 fusion
  194.1 0.0 copy-start.1
  194.1 1.8 copy.14
  195.9 0.0 copy-done.1
  195.9 0.0 copy-start
  195.9 0.8 copy.15
  196.7 0.4 copy-done
  197.1 0.8 copy.16
  (2 shorter events, 0.0 us)
Async XLA Ops:
  1.4 0.7 copy-start.3
  2.1 0.7 copy-start.2
  194.1 1.8 copy-start.1
  195.9 1.1 copy-start
